TPU v7x, 32 devices: a whole 2x2x4 slice. The times are simulated.
32 devices in a mesh: ctx: 8 (over y, x, core), shard: 4 (over z).
Axes of the slice: x: 2, y: 2, z: 4, core: 2. Of those that a mesh axis runs over, the one named last changes fastest.
Arguments:
- layer_input: bfloat16 [2, 4096, 768], P(None, ('ctx', 'shard')), may hold values from -6 to 6
- attn_gain: bfloat16 [768], P('shard'), may hold values from 0.099609375 to 1.8984375
- attn_shift: bfloat16 [768], P('shard'), may hold values from -3 to 3
- qkv_weight: bfloat16 [768, 2304], P('shard'), may hold values from -0.3125 to 0.3125
- query_bias: bfloat16 [768], P('shard'), may hold values from -3 to 3
- value_bias: bfloat16 [768], P('shard'), may hold values from -3 to 3
- proj_weight: bfloat16 [768, 768], P('shard'), may hold values from -3.5 to 3.5
- proj_bias: bfloat16 [768], P('shard'), may hold values from -1.75 to 1.75
- mlp_gain: bfloat16 [768], P('shard'), may hold values from 0.099609375 to 1.8984375
- mlp_shift: bfloat16 [768], P('shard'), may hold values from -3 to 3
- fc_weight: bfloat16 [768, 3072], P('shard'), may hold values from -0.21875 to 0.21875
- fc_bias: bfloat16 [3072], P('shard'), may hold values from -3 to 3
- out_weight: bfloat16 [3072, 768], P('shard'), may hold values from -0.109375 to 0.109375
- out_bias: bfloat16 [768], P('shard'), may hold values from -1.75 to 1.75
- grad_output: bfloat16 [2, 4096, 768], P(None, ('ctx', 'shard')), may hold values from -6 to 6
Outputs:
- layer_output: bfloat16 [2, 4096, 768], P(None, ('ctx', 'shard'))
- input_grad: bfloat16 [2, 4096, 768], P(None, ('ctx', 'shard'))
- attn_gain_grad: float32 [768], P('shard')
- attn_shift_grad: float32 [768], P('shard')
- qkv_weight_grad: float32 [768, 2304], P('shard')
- query_bias_grad: float32 [768], P('shard')
- value_bias_grad: float32 [768], P('shard')
- proj_weight_grad: float32 [768, 768], P('shard')
- proj_bias_grad: float32 [768], P('shard')
- mlp_gain_grad: float32 [768], P('shard')
- mlp_shift_grad: float32 [768], P('shard')
- fc_weight_grad: float32 [768, 3072], P('shard')
- fc_bias_grad: float32 [3072], P('shard')
- out_weight_grad: float32 [3072, 768], P('shard')
- out_bias_grad: float32 [768], P('shard')
All inputs are finite; a program needn't handle non-finite values.
Results may differ from a plain program's by a relative error of at most 0.014.
The roundings to bfloat16 on the way count: a program that leaves them out, or rounds other values in their place, can miss the bound.
Values may be sent and summed in bfloat16 or wider, within the bound.
No kernel may reach another device: no remote copies, remote signals or barrier semaphores. Data moves between devices by JAX's collectives and lax.ppermute only.
A program may use at most 256 MiB of HBM per device.

v0:
```python
import jax
import jax.numpy as jnp
from jax import lax
from jax.sharding import PartitionSpec as P

HEADS = 12
HEAD = 64


def passed_along(block, axis, distance):
    devices = range(lax.axis_size(axis))
    route = [((i - distance) % len(devices), i) for i in devices]
    return lax.ppermute(block, axis, route)


def combined_all(part, axis, combine):
    gathered = jax.tree.map(lambda a: lax.all_gather(a, axis), part)

    def take(source):
        return jax.tree.map(lambda a: lax.dynamic_index_in_dim(a, source, 0, False), gathered)

    return lax.fori_loop(
        1, lax.axis_size(axis), lambda source, state: combine(state, take(source)), take(0)
    )


def layer_norm(values, gain, shift):
    centered = values - jnp.mean(values, axis=-1, keepdims=True)
    variance = jnp.mean(centered * centered, axis=-1, keepdims=True)
    return centered * lax.rsqrt(variance + 1e-05) * gain + shift


def gelu_tanh(values):
    return jax.nn.gelu(values, approximate=True)


def join_stats(first, second):
    newmax = jnp.maximum(first[1], second[1])
    factor_one = jnp.exp(first[1] - newmax)
    factor_two = jnp.exp(second[1] - newmax)
    totals = first[0] * factor_one[..., None] + second[0] * factor_two[..., None]
    return (totals, newmax, first[2] * factor_one + second[2] * factor_two)


def move_grads(key_sums, value_sums):
    return passed_along((key_sums, value_sums), "ctx", 1)


def token_places(ctx_owner, shard_ids, within, row_count, block_rows, cycle_size):
    piece = row_count // cycle_size
    return within // piece * block_rows + shard_ids * row_count + ctx_owner * piece + within % piece


def body(
    layer_input,
    attn_gain,
    attn_shift,
    qkv_weight,
    query_bias,
    value_bias,
    proj_weight,
    proj_bias,
    mlp_gain,
    mlp_shift,
    fc_weight,
    fc_bias,
    out_weight,
    out_bias,
    grad_output,
):
    f32 = jnp.float32
    bf16 = jnp.bfloat16
    layer_input, grad_output = (
        lax.all_to_all(layer_input, "ctx", split_axis=1, concat_axis=1, tiled=True),
        lax.all_to_all(grad_output, "ctx", split_axis=1, concat_axis=1, tiled=True),
    )
    gathered = (
        lax.all_gather(attn_gain, "shard", axis=0, tiled=True),
        lax.all_gather(attn_shift, "shard", axis=0, tiled=True),
        lax.all_gather(qkv_weight, "shard", axis=0, tiled=True),
        lax.all_gather(query_bias, "shard", axis=0, tiled=True),
        lax.all_gather(value_bias, "shard", axis=0, tiled=True),
        lax.all_gather(proj_weight, "shard", axis=0, tiled=True),
        lax.all_gather(proj_bias, "shard", axis=0, tiled=True),
        lax.all_gather(mlp_gain, "shard", axis=0, tiled=True),
        lax.all_gather(mlp_shift, "shard", axis=0, tiled=True),
        lax.all_gather(fc_weight, "shard", axis=0, tiled=True),
        lax.all_gather(fc_bias, "shard", axis=0, tiled=True),
        lax.all_gather(out_weight, "shard", axis=0, tiled=True),
        lax.all_gather(out_bias, "shard", axis=0, tiled=True),
    )
    gain_one = gathered[0].astype(f32)
    shift_one = gathered[1].astype(f32)
    query_key_value_full = gathered[2]
    query_add = gathered[3].astype(f32)
    value_add = gathered[4].astype(f32)
    projection_full_weight = gathered[5]
    projection_bias_added = gathered[6].astype(f32)
    gain_two = gathered[7].astype(f32)
    shift_two = gathered[8].astype(f32)
    feedforward_full_weight = gathered[9]
    feedforward_bias_added = gathered[10].astype(f32)
    output_full_weight = gathered[11]
    output_bias_added = gathered[12].astype(f32)
    seq_count, row_count, width = layer_input.shape
    head_count = HEADS
    head_size = HEAD
    ctx_place = lax.axis_index("ctx")
    shard_place = lax.axis_index("shard")
    cycle_size = lax.axis_size("ctx")
    block_rows = row_count * lax.axis_size("shard")
    inputs32 = layer_input.astype(f32)
    first_normed_input = layer_norm(inputs32, gain_one, shift_one).astype(bf16)
    projected_output = jnp.einsum(
        "srd,de->sre", first_normed_input, query_key_value_full, preferred_element_type=f32
    )
    queries = (projected_output[..., :width] + query_add).astype(bf16)
    keys_own = (
        projected_output[..., width : 2 * width]
        .astype(bf16)
        .reshape(seq_count, row_count, head_count, head_size)
    )
    values_own = (
        (projected_output[..., 2 * width :] + value_add)
        .astype(bf16)
        .reshape(seq_count, row_count, head_count, head_size)
    )
    query_block = lax.all_gather(queries, "shard", axis=1, tiled=True).reshape(
        seq_count, block_rows, head_count, head_size
    )
    block_index = jnp.arange(block_rows)
    query_places = token_places(
        ctx_place,
        block_index // row_count,
        block_index % row_count,
        row_count,
        block_rows,
        cycle_size,
    )
    row_index = jnp.arange(row_count)

    def masked_scores(key_tile, source):
        key_places = token_places(source, shard_place, row_index, row_count, block_rows, cycle_size)
        allowed = key_places[None, :] <= query_places[:, None]
        scores = (
            jnp.einsum("sqhd,skhd->shqk", query_block, key_tile, preferred_element_type=f32) * 0.125
        )
        return (jnp.where(allowed, scores, -1e30), allowed)

    def forward_step(carried, key_tile, value_tile, source):
        totals, running, normal = carried
        scores, allowed = masked_scores(key_tile, source)
        newmax = jnp.maximum(running, jnp.max(scores, axis=-1))
        factor = jnp.exp(running - newmax)
        weights = jnp.where(allowed, jnp.exp(scores - newmax[..., None]), 0.0)
        normal = normal * factor + jnp.sum(weights, axis=-1)
        totals = totals * factor[..., None] + jnp.einsum(
            "shqk,skhd->shqd", weights.astype(bf16), value_tile, preferred_element_type=f32
        )
        return (totals, newmax, normal)

    start_stats = (
        jnp.zeros((seq_count, head_count, block_rows, head_size), f32),
        jnp.full((seq_count, head_count, block_rows), -1e30, f32),
        jnp.zeros((seq_count, head_count, block_rows), f32),
    )
    carried = forward_step(start_stats, keys_own, values_own, ctx_place)

    def cycle_turn(turn_index, state):
        stats, key_tile, value_tile = state
        key_tile, value_tile = passed_along((key_tile, value_tile), "ctx", 1)
        source = (ctx_place - turn_index) % cycle_size
        stats = forward_step(stats, key_tile, value_tile, source)
        return (stats, key_tile, value_tile)

    carried, spent_keys, spent_values = lax.fori_loop(
        1, cycle_size, cycle_turn, (carried, keys_own, values_own)
    )
    joined = combined_all((carried[0], carried[1], carried[2]), "shard", join_stats)
    first_row = shard_place * row_count
    totals = lax.dynamic_slice_in_dim(joined[0], first_row, row_count, 2)
    running = lax.dynamic_slice_in_dim(joined[1], first_row, row_count, 2)
    normal = lax.dynamic_slice_in_dim(joined[2], first_row, row_count, 2)
    attention_output = totals / normal[..., None]
    log_total = running + jnp.log(normal)
    attended32 = attention_output.transpose(0, 2, 1, 3).reshape(seq_count, row_count, width)
    attended_low = attended32.astype(bf16)
    residual_branch = (
        jnp.einsum("srd,de->sre", attended_low, projection_full_weight, preferred_element_type=f32)
        + projection_bias_added
    )
    middle_state = inputs32 + residual_branch
    second_normed_input = layer_norm(middle_state, gain_two, shift_two).astype(bf16)
    preactivation_values = (
        jnp.einsum(
            "srd,df->srf", second_normed_input, feedforward_full_weight, preferred_element_type=f32
        )
        + feedforward_bias_added
    )
    hidden_state = gelu_tanh(preactivation_values).astype(bf16)
    output32 = (
        middle_state
        + jnp.einsum("srf,fd->srd", hidden_state, output_full_weight, preferred_element_type=f32)
        + output_bias_added
    )
    layer_output = output32.astype(bf16)
    grad32 = grad_output.astype(f32)
    out_grad = jnp.einsum("srf,srd->fd", hidden_state, grad_output, preferred_element_type=f32)
    out_add_grad = jnp.sum(grad32, axis=(0, 1))
    grad_hidden = jnp.einsum(
        "srd,fd->srf", grad_output, output_full_weight, preferred_element_type=f32
    )
    gelu_pull = jax.vjp(gelu_tanh, preactivation_values)[1]
    grad_pre = gelu_pull(grad_hidden)[0].astype(bf16)
    fc_grad = jnp.einsum("srd,srf->df", second_normed_input, grad_pre, preferred_element_type=f32)
    fc_add_grad = jnp.sum(grad_pre.astype(f32), axis=(0, 1))
    grad_normed_two = jnp.einsum(
        "srf,df->srd", grad_pre, feedforward_full_weight, preferred_element_type=f32
    )
    norm_two_pull = jax.vjp(layer_norm, middle_state, gain_two, shift_two)[1]
    grad_mid_part, gain_two_grad, shift_two_grad = norm_two_pull(grad_normed_two)
    grad_middle = grad32 + grad_mid_part
    grad_branch = grad_middle.astype(bf16)
    proj_grad = jnp.einsum("srd,sre->de", attended_low, grad_branch, preferred_element_type=f32)
    proj_add_grad = jnp.sum(grad_branch.astype(f32), axis=(0, 1))
    grad_attended = jnp.einsum(
        "sre,de->srd", grad_branch, projection_full_weight, preferred_element_type=f32
    ).astype(bf16)
    grad_four = grad_attended.reshape(seq_count, row_count, head_count, head_size)
    deltas = jnp.sum(
        grad_four.astype(f32) * attended32.reshape(seq_count, row_count, head_count, head_size),
        axis=-1,
    ).transpose(0, 2, 1)
    grad_block = lax.all_gather(grad_attended, "shard", axis=1, tiled=True).reshape(
        seq_count, block_rows, head_count, head_size
    )
    delta_block, log_block = (
        lax.all_gather(deltas, "shard", axis=2, tiled=True),
        lax.all_gather(log_total, "shard", axis=2, tiled=True),
    )

    def backward_step(sums, key_tile, value_tile, source):
        query_sums, key_sums, value_sums = sums
        scores, allowed = masked_scores(key_tile, source)
        weights = jnp.where(allowed, jnp.exp(scores - log_block[..., None]), 0.0)
        pulled = jnp.einsum("sqhd,skhd->shqk", grad_block, value_tile, preferred_element_type=f32)
        slopes = (weights * (pulled - delta_block[..., None])).astype(bf16)
        query_sums = query_sums + 0.125 * jnp.einsum(
            "shqk,skhd->sqhd", slopes, key_tile, preferred_element_type=f32
        )
        key_sums = key_sums + 0.125 * jnp.einsum(
            "shqk,sqhd->skhd", slopes, query_block, preferred_element_type=f32
        )
        value_sums = value_sums + jnp.einsum(
            "shqk,sqhd->skhd", weights.astype(bf16), grad_block, preferred_element_type=f32
        )
        return (query_sums, key_sums, value_sums)

    zero_rows = jnp.zeros((seq_count, row_count, head_count, head_size), f32)
    start_sums = (
        jnp.zeros((seq_count, block_rows, head_count, head_size), f32),
        zero_rows,
        zero_rows,
    )
    sums = backward_step(start_sums, keys_own, values_own, ctx_place)

    def back_turn(turn_index, state):
        query_sums, key_sums, value_sums, key_tile, value_tile = state
        key_tile, value_tile = passed_along((key_tile, value_tile), "ctx", 1)
        key_sums, value_sums = move_grads(key_sums, value_sums)
        source = (ctx_place - turn_index) % cycle_size
        current = backward_step((query_sums, key_sums, value_sums), key_tile, value_tile, source)
        return (current[0], current[1], current[2], key_tile, value_tile)

    ended = lax.fori_loop(
        1, cycle_size, back_turn, (sums[0], sums[1], sums[2], keys_own, values_own)
    )
    key_sums, value_sums = move_grads(ended[1], ended[2])
    query_grad = lax.psum_scatter(ended[0], "shard", scatter_dimension=1, tiled=True)
    query_low = query_grad.reshape(seq_count, row_count, width).astype(bf16)
    key_low = key_sums.reshape(seq_count, row_count, width).astype(bf16)
    value_low = value_sums.reshape(seq_count, row_count, width).astype(bf16)
    grad_qkv = jnp.concatenate([query_low, key_low, value_low], axis=-1)
    qkv_grad = jnp.einsum("srd,sre->de", first_normed_input, grad_qkv, preferred_element_type=f32)
    query_add_grad = jnp.sum(query_low.astype(f32), axis=(0, 1))
    value_add_grad = jnp.sum(value_low.astype(f32), axis=(0, 1))
    grad_normed_one = jnp.einsum(
        "sre,de->srd", grad_qkv, query_key_value_full, preferred_element_type=f32
    )
    norm_one_pull = jax.vjp(layer_norm, inputs32, gain_one, shift_one)[1]
    grad_in_part, gain_one_grad, shift_one_grad = norm_one_pull(grad_normed_one)
    input_grad = (grad_middle + grad_in_part).astype(bf16)
    layer_output, input_grad = (
        lax.all_to_all(layer_output, "ctx", split_axis=1, concat_axis=1, tiled=True),
        lax.all_to_all(input_grad, "ctx", split_axis=1, concat_axis=1, tiled=True),
    )
    summed = lax.psum(
        (
            gain_one_grad,
            shift_one_grad,
            qkv_grad,
            query_add_grad,
            value_add_grad,
            proj_grad,
            proj_add_grad,
            gain_two_grad,
            shift_two_grad,
            fc_grad,
            fc_add_grad,
            out_grad,
            out_add_grad,
        ),
        "ctx",
    )
    shards = (
        lax.psum_scatter(summed[0], "shard", scatter_dimension=0, tiled=True),
        lax.psum_scatter(summed[1], "shard", scatter_dimension=0, tiled=True),
        lax.psum_scatter(summed[2], "shard", scatter_dimension=0, tiled=True),
        lax.psum_scatter(summed[3], "shard", scatter_dimension=0, tiled=True),
        lax.psum_scatter(summed[4], "shard", scatter_dimension=0, tiled=True),
        lax.psum_scatter(summed[5], "shard", scatter_dimension=0, tiled=True),
        lax.psum_scatter(summed[6], "shard", scatter_dimension=0, tiled=True),
        lax.psum_scatter(summed[7], "shard", scatter_dimension=0, tiled=True),
        lax.psum_scatter(summed[8], "shard", scatter_dimension=0, tiled=True),
        lax.psum_scatter(summed[9], "shard", scatter_dimension=0, tiled=True),
        lax.psum_scatter(summed[10], "shard", scatter_dimension=0, tiled=True),
        lax.psum_scatter(summed[11], "shard", scatter_dimension=0, tiled=True),
        lax.psum_scatter(summed[12], "shard", scatter_dimension=0, tiled=True),
    )
    return (
        layer_output,
        input_grad,
        shards[0],
        shards[1],
        shards[2],
        shards[3],
        shards[4],
        shards[5],
        shards[6],
        shards[7],
        shards[8],
        shards[9],
        shards[10],
        shards[11],
        shards[12],
    )


def solution(mesh):
    return jax.shard_map(
        body,
        mesh=mesh,
        in_specs=(
            P(None, ("ctx", "shard"), None),
            P("shard"),
            P("shard"),
            P("shard", None),
            P("shard"),
            P("shard"),
            P("shard", None),
            P("shard"),
            P("shard"),
            P("shard"),
            P("shard", None),
            P("shard"),
            P("shard", None),
            P("shard"),
            P(None, ("ctx", "shard"), None),
        ),
        out_specs=(
            P(None, ("ctx", "shard"), None),
            P(None, ("ctx", "shard"), None),
            P("shard"),
            P("shard"),
            P("shard", None),
            P("shard"),
            P("shard"),
            P("shard", None),
            P("shard"),
            P("shard"),
            P("shard"),
            P("shard", None),
            P("shard"),
            P("shard", None),
            P("shard"),
        ),
        check_vma=False,
    )
```

profile of v0, /device:TPU:0, one launch (start us, length us, event | category | flops | bytes accessed | tf_op | source)
XLA Modules:
  0.0 1699.6 jit_solution(15470523215416914629)
XLA Ops:
  24.0 20.2 %all-reduce.20 = (bf16[768]{0:T(1024)(128)(2,1)S(1)}, bf16[768]{0:T(1024)(128)(2,1)S(1)}, bf16[768]{0:T(1024)(128)(2,1)S(1)}, bf16[768]{0:T(1024)(128)(2,1)S(1)}...) all-reduce(bf16[768]{0:T(1024)(128)(2,1)S(1)} %dynamic-update-slice, ...), channel_id=1, replica_groups=mesh['ctx'=8,'shard'=4] {'shard'}, use_global_device_ids=true, to_apply=%add.1 | all-reduce | flops 6144 | bytes 24576
  44.7 38.1 %all-gather.12.cloned.1.call-done = bf16[768,2304]{1,0:T(8,128)(2,1)} async-done(((bf16[192,2304]{1,0:T(8,128)(2,1)}), bf16[768,2304]{1,0:T(8,128)(2,1)}) %all-gather.12.cloned.1.call-update) | async-done | bytes 3538960 | tf_op jit(solution)/shard_map/all_gather | solution.py:80
  94.5 29.6 %all-gather.14.cloned.1.call-done = bf16[2,512,768]{2,1,0:T(8,128)(2,1)} async-done(((bf16[2,128,768]{2,1,0:T(8,128)(2,1)}), bf16[2,512,768]{2,1,0:T(8,128)(2,1)}) %all-gather.14.cloned.1.call-update) | async-done | bytes 1572880 | tf_op jit(solution)/shard_map/all_gather | solution.py:128
  135.3 115.4 %while.74 = (s32[]{:T(128)}, f32[2,12,512,64]{2,3,1,0:T(8,128)}, f32[2,12,512]{2,1,0:T(8,128)S(1)}, f32[2,12,512]{2,1,0:T(8,128)S(1)}, bf16[2,128,12,64]{1,3,2,0...) while((s32[]{:T(128)}, f32[2,12,512,64]{2,3,1,0:T(8,128)}, ...), condition=%wide.region_7.8_spmd.clone.clone, body=%wide.region_4.7_spmd.clone.clone.sunk | while | flops 424783872 | bytes 58463652 | solution.py:176
  257.3 13.2 all-gather.3
  271.1 18.4 %all-gather.1 = f32[8,12,512]{2,1,0:T(8,128)S(1)} all-gather(f32[2,12,512]{2,1,0:T(8,128)S(1)} %get-tuple-element.1054), channel_id=3, replica_groups=mesh['ctx'=8,'shard'=4] {'shard'}, dimensions={0}, use_global_device_ids=true | all-gather | bytes 245760 | tf_op jit(solution)/shard_map/all_gather | solution.py:17
  289.5 22.4 %all-gather.2 = f32[8,12,512]{2,1,0:T(8,128)S(1)} all-gather(f32[2,12,512]{2,1,0:T(8,128)S(1)} %get-tuple-element.1055), channel_id=4, replica_groups=mesh['ctx'=8,'shard'=4] {'shard'}, dimensions={0}, use_global_device_ids=true | all-gather | bytes 245760 | tf_op jit(solution)/shard_map/all_gather | solution.py:17
  312.0 163.6 %all-gather.24.cloned.1.call-done = f32[8,12,512,64]{2,3,1,0:T(8,128)} async-done(((f32[2,12,512,64]{2,3,1,0:T(8,128)}), f32[8,12,512,64]{2,3,1,0:T(8,128)}) %all-gather.24.cloned.1.call-update) | async-done | bytes 12582928 | tf_op jit(solution)/shard_map/all_gather | solution.py:17
  485.4 59.3 %while.73 = (s32[]{:T(128)}, f32[2,12,512,64]{3,2,1,0:T(8,128)}, f32[2,12,512]{2,1,0:T(8,128)S(1)}, f32[2,12,512]{2,1,0:T(8,128)S(1)}, f32[4,2,12,512]{3,2,1,0:T...) while((s32[]{:T(128)}, f32[2,12,512,64]{3,2,1,0:T(8,128)}, ...), condition=%wide.region_9.10_spmd, body=%wide.region_8.9_spmd.sunk | while | flops 2433029 | bytes 22511768 | solution.py:22
  515.1 9.9 fusion.260
  535.0 9.7 fusion.260
  556.2 39.5 %all-gather.18.cloned.1.call-done = bf16[768,3072]{1,0:T(8,128)(2,1)} async-done(((bf16[192,3072]{1,0:T(8,128)(2,1)}), bf16[768,3072]{1,0:T(8,128)(2,1)}) %all-gather.18.cloned.1.call-update) | async-done | bytes 4718608 | tf_op jit(solution)/shard_map/all_gather | solution.py:87
  601.2 83.8 %all-gather.20.cloned.1.call-done = bf16[3072,768]{1,0:T(8,128)(2,1)} async-done(((bf16[768,768]{1,0:T(8,128)(2,1)}), bf16[3072,768]{1,0:T(8,128)(2,1)}) %all-gather.20.cloned.1.call-update) | async-done | bytes 4718608 | tf_op jit(solution)/shard_map/all_gather | solution.py:89
  702.1 13.8 all_gather.89
  717.3 14.3 all_gather.91
  756.1 240.2 %while.75 = (s32[]{:T(128)}, f32[2,512,12,64]{1,3,2,0:T(8,128)}, f32[2,128,12,64]{1,3,2,0:T(8,128)}, f32[2,128,12,64]{1,3,2,0:T(8,128)}, bf16[2,128,12,64]{1,3,2...) while((s32[]{:T(128)}, f32[2,512,12,64]{1,3,2,0:T(8,128)}, ...), condition=%wide.region_16.17_spmd.clone.clone, body=%wide.region_15.16_spmd.clone.clone.sunk | while | flops 1027756032 | bytes 88823456 | solution.py:275
  1028.9 25.9 %reduce-scatter.6.cloned.1.call-done = f32[2,128,12,64]{1,3,2,0:T(8,128)} async-done(((f32[2,512,12,64]{1,3,2,0:T(8,128)}), f32[2,128,12,64]{1,3,2,0:T(8,128)}) %reduce-scatter.6.cloned.1.call-update) | async-done | bytes 786448 | tf_op jit(solution)/shard_map/reduce_scatter | solution.py:279
  1061.3 44.5 %reduce-scatter.10.cloned.1.call-done = f32[192,768]{1,0:T(8,128)} async-done(((f32[768,768]{1,0:T(8,128)}), f32[192,768]{1,0:T(8,128)}) %reduce-scatter.10.cloned.1.call-update) | async-done | bytes 589840 | tf_op jit(solution)/shard_map/reduce_scatter | solution.py:321
  1105.8 163.0 %reduce-scatter.12.cloned.1.call-done = f32[192,3072]{1,0:T(8,128)} async-done(((f32[768,3072]{1,0:T(8,128)}), f32[192,3072]{1,0:T(8,128)}) %reduce-scatter.12.cloned.1.call-update) | async-done | bytes 2359312 | tf_op jit(solution)/shard_map/reduce_scatter | solution.py:325
  1268.9 164.5 %reduce-scatter.14.cloned.1.call-done = f32[768,768]{1,0:T(8,128)} async-done(((f32[3072,768]{1,0:T(8,128)}), f32[768,768]{1,0:T(8,128)}) %reduce-scatter.14.cloned.1.call-update) | async-done | bytes 2359312 | tf_op jit(solution)/shard_map/reduce_scatter | solution.py:327
  1433.4 126.5 %reduce-scatter.8.cloned.1.call-done = f32[192,2304]{1,0:T(8,128)} async-done(((f32[768,2304]{1,0:T(8,128)}), f32[192,2304]{1,0:T(8,128)}) %reduce-scatter.8.cloned.1.call-update) | async-done | bytes 1769488 | tf_op jit(solution)/shard_map/reduce_scatter | solution.py:318
  1589.4 19.0 %all-reduce.19 = (f32[768]{0:T(1024)S(1)}, f32[768]{0:T(1024)S(1)}, f32[768]{0:T(1024)S(1)}, f32[768]{0:T(1024)S(1)}, f32[768]{0:T(1024)S(1)}, /*index=5*/f32[76...) all-reduce(f32[768]{0:T(1024)S(1)} %get-tuple-element.1253, ...), channel_id=6, replica_groups=mesh['ctx'=8,'shard'=4] {'shard'}, use_global_device_ids=true, to_apply=%region_22.23.clone | all-reduce | flops 9216 | bytes 73728
  1609.1 22.8 %all-reduce.17 = (f32[192]{0:T(256)}, f32[192]{0:T(256)}, f32[192]{0:T(256)}, f32[192]{0:T(256)}, f32[192]{0:T(256)}, /*index=5*/f32[192]{0:T(256)}, f32[192]{0:T(256)}, f32[768]{0:T(1024)}, f32[192]{0:T(256)}) all-reduce(f32[192]{0:T(256)S(1)} %dynamic-slice.9, ...), channel_id=1, replica_groups=mesh['ctx'=8,'shard'=4] {'ctx'}, use_global_device_ids=true, to_apply=%region_21.22 | all-reduce | flops 2304 | bytes 18432 | tf_op jit(solution)/shard_map/psum | solution.py:297
  1632.7 53.6 %all-reduce.23.cloned.1.call-done = (f32[192,2304]{1,0:T(8,128)}, f32[192,768]{1,0:T(8,128)}, f32[192,3072]{1,0:T(8,128)}, f32[768,768]{1,0:T(8,128)}) async-done(((f32[192,2304]{1,0:T(8,128)}, f32[192,768]{1,0:T(8,128)}, f32[192,3072]{1,0:T(8,128)}, f32[768,768]{1,0:T(8,128)}), (f32[192,2304]{1,0:T(8,128)}, f32[192,768]{1,0:T(8,128)}, f32[192,3072]{1,0:T(8,128)}, ...) | async-done | bytes 7077904 | tf_op jit(solution)/shard_map/psum | solution.py:297
  (614 shorter events, 585.2 us)
Async XLA Ops:
  7.2 75.6 %all-gather.12.cloned.1.call-start = ((), (), s32[]{:S(2)}) async-start(), calls=%async_computation.9 | async-start | bytes 4423680 | tf_op jit(solution)/shard_map/all_gather | solution.py:80
  10.1 34.2 %all-to-all-start = ((bf16[2,128,768]{2,0,1:T(2,128)(2,1)}), bf16[2,128,768]{2,0,1:T(2,128)(2,1)S(1)}, u32[]{:S(2)}, u32[]{:S(2)}) async-start(bf16[2,128,768]{2,0,1:T(2,128)(2,1)} %copy.83), calls=%async_computation | async-start | bytes 786432 | tf_op jit(solution)/shard_map/all_to_all | solution.py:74
  15.2 108.9 %all-gather.14.cloned.1.call-start = ((), (), s32[]{:S(2)}) async-start(), calls=%async_computation.10 | async-start | bytes 1966080 | tf_op jit(solution)/shard_map/all_gather | solution.py:128
  88.3 387.3 %all-gather.24.cloned.1.call-start = ((), (), s32[]{:S(2)}) async-start(), calls=%async_computation.16 | async-start | bytes 15728640 | tf_op jit(solution)/shard_map/all_gather | solution.py:17
  250.8 302.6 %all-gather.16.cloned.1.call-start = ((), (), s32[]{:S(2)}) async-start(), calls=%async_computation.11 | async-start | bytes 1474560 | tf_op jit(solution)/shard_map/all_gather | solution.py:83
  251.4 344.3 %all-gather.18.cloned.1.call-start = ((), (), s32[]{:S(2)}) async-start(), calls=%async_computation.12 | async-start | bytes 5898240 | tf_op jit(solution)/shard_map/all_gather | solution.py:87
  251.9 433.1 %all-gather.20.cloned.1.call-start = ((), (), s32[]{:S(2)}) async-start(), calls=%async_computation.13 | async-start | bytes 5898240 | tf_op jit(solution)/shard_map/all_gather | solution.py:89
  253.7 347.5 %all-to-all-start.2 = ((bf16[2,128,768]{2,0,1:T(2,128)(2,1)}), bf16[2,128,768]{2,0,1:T(2,128)(2,1)S(1)}, u32[]{:S(2)}, u32[]{:S(2)}) async-start(bf16[2,128,768]{2,0,1:T(2,128)(2,1)} %copy.94), calls=%async_computation.2 | async-start | bytes 786432 | tf_op jit(solution)/shard_map/all_to_all | solution.py:75
  257.2 480.8 %all-gather.22.cloned.1.call-start = ((), (), s32[]{:S(2)}) async-start(), calls=%async_computation.14 | async-start | bytes 1966080 | tf_op jit(solution)/shard_map/all_gather | solution.py:234
  700.9 353.9 %reduce-scatter.6.cloned.1.call-start = ((), (), s32[]{:S(2)}) async-start(), calls=%async_computation.15 | async-start | bytes 3932160 | tf_op jit(solution)/shard_map/reduce_scatter | solution.py:279
  757.8 27.8 %collective-permute-start.5 = (f32[2,128,12,64]{1,3,2,0:T(8,128)}, f32[2,128,12,64]{1,3,2,0:T(8,128)}, u32[]{:S(2)}, u32[]{:S(2)}) collective-permute-start(f32[2,128,12,64]{1,3,2,0:T(8,128)} %get-tuple-element.1675), channel_id=1, source_target_pairs={{28,0},{0,4},{4,8},{8,12},{12,16},{16,20},{20,24},{24,28},{29,1},{... | collective-permute-start | bytes 2359304 | tf_op jit(solution)/shard_map/while/body/eval_jaxpr/ppermute | solution.py:13
  791.2 28.7 %collective-permute-start.5 = (f32[2,128,12,64]{1,3,2,0:T(8,128)}, f32[2,128,12,64]{1,3,2,0:T(8,128)}, u32[]{:S(2)}, u32[]{:S(2)}) collective-permute-start(f32[2,128,12,64]{1,3,2,0:T(8,128)} %get-tuple-element.1675), channel_id=1, source_target_pairs={{28,0},{0,4},{4,8},{8,12},{12,16},{16,20},{20,24},{24,28},{29,1},{... | collective-permute-start | bytes 2359304 | tf_op jit(solution)/shard_map/while/body/eval_jaxpr/ppermute | solution.py:13
  825.4 28.9 %collective-permute-start.5 = (f32[2,128,12,64]{1,3,2,0:T(8,128)}, f32[2,128,12,64]{1,3,2,0:T(8,128)}, u32[]{:S(2)}, u32[]{:S(2)}) collective-permute-start(f32[2,128,12,64]{1,3,2,0:T(8,128)} %get-tuple-element.1675), channel_id=1, source_target_pairs={{28,0},{0,4},{4,8},{8,12},{12,16},{16,20},{20,24},{24,28},{29,1},{... | collective-permute-start | bytes 2359304 | tf_op jit(solution)/shard_map/while/body/eval_jaxpr/ppermute | solution.py:13
  859.7 21.1 %collective-permute-start.4 = (f32[2,128,12,64]{1,3,2,0:T(8,128)}, f32[2,128,12,64]{1,3,2,0:T(8,128)S(1)}, u32[]{:S(2)}, u32[]{:S(2)}) collective-permute-start(f32[2,128,12,64]{1,3,2,0:T(8,128)} %get-tuple-element.1674), channel_id=1, source_target_pairs={{28,0},{0,4},{4,8},{8,12},{12,16},{16,20},{20,24},{24,28},{29,1},{... | collective-permute-start | bytes 2359304 | tf_op jit(solution)/shard_map/while/body/eval_jaxpr/ppermute | solution.py:13
  859.7 28.9 %collective-permute-start.5 = (f32[2,128,12,64]{1,3,2,0:T(8,128)}, f32[2,128,12,64]{1,3,2,0:T(8,128)}, u32[]{:S(2)}, u32[]{:S(2)}) collective-permute-start(f32[2,128,12,64]{1,3,2,0:T(8,128)} %get-tuple-element.1675), channel_id=1, source_target_pairs={{28,0},{0,4},{4,8},{8,12},{12,16},{16,20},{20,24},{24,28},{29,1},{... | collective-permute-start | bytes 2359304 | tf_op jit(solution)/shard_map/while/body/eval_jaxpr/ppermute | solution.py:13
  894.0 28.9 %collective-permute-start.5 = (f32[2,128,12,64]{1,3,2,0:T(8,128)}, f32[2,128,12,64]{1,3,2,0:T(8,128)}, u32[]{:S(2)}, u32[]{:S(2)}) collective-permute-start(f32[2,128,12,64]{1,3,2,0:T(8,128)} %get-tuple-element.1675), channel_id=1, source_target_pairs={{28,0},{0,4},{4,8},{8,12},{12,16},{16,20},{20,24},{24,28},{29,1},{... | collective-permute-start | bytes 2359304 | tf_op jit(solution)/shard_map/while/body/eval_jaxpr/ppermute | solution.py:13
  928.4 28.9 %collective-permute-start.5 = (f32[2,128,12,64]{1,3,2,0:T(8,128)}, f32[2,128,12,64]{1,3,2,0:T(8,128)}, u32[]{:S(2)}, u32[]{:S(2)}) collective-permute-start(f32[2,128,12,64]{1,3,2,0:T(8,128)} %get-tuple-element.1675), channel_id=1, source_target_pairs={{28,0},{0,4},{4,8},{8,12},{12,16},{16,20},{20,24},{24,28},{29,1},{... | collective-permute-start | bytes 2359304 | tf_op jit(solution)/shard_map/while/body/eval_jaxpr/ppermute | solution.py:13
  962.7 28.9 %collective-permute-start.5 = (f32[2,128,12,64]{1,3,2,0:T(8,128)}, f32[2,128,12,64]{1,3,2,0:T(8,128)}, u32[]{:S(2)}, u32[]{:S(2)}) collective-permute-start(f32[2,128,12,64]{1,3,2,0:T(8,128)} %get-tuple-element.1675), channel_id=1, source_target_pairs={{28,0},{0,4},{4,8},{8,12},{12,16},{16,20},{20,24},{24,28},{29,1},{... | collective-permute-start | bytes 2359304 | tf_op jit(solution)/shard_map/while/body/eval_jaxpr/ppermute | solution.py:13
  996.4 109.4 %reduce-scatter.10.cloned.1.call-start = ((), (), s32[]{:S(2)}) async-start(), calls=%async_computation.18 | async-start | bytes 2949120 | tf_op jit(solution)/shard_map/reduce_scatter | solution.py:321
  999.4 269.5 %reduce-scatter.12.cloned.1.call-start = ((), (), s32[]{:S(2)}) async-start(), calls=%async_computation.19 | async-start | bytes 11796480 | tf_op jit(solution)/shard_map/reduce_scatter | solution.py:325
  1006.4 427.0 %reduce-scatter.14.cloned.1.call-start = ((), (), s32[]{:S(2)}) async-start(), calls=%async_computation.20 | async-start | bytes 11796480 | tf_op jit(solution)/shard_map/reduce_scatter | solution.py:327
  1015.3 544.6 %reduce-scatter.8.cloned.1.call-start = ((), (), s32[]{:S(2)}) async-start(), calls=%async_computation.17 | async-start | bytes 8847360 | tf_op jit(solution)/shard_map/reduce_scatter | solution.py:318
  1061.3 625.0 %all-reduce.23.cloned.1.call-start = ((), (), s32[]{:S(2)}) async-start(), calls=%async_computation.21 | async-start | bytes 14155776 | tf_op jit(solution)/shard_map/psum | solution.py:297
  1583.5 48.4 %all-to-all-start.3 = ((bf16[2,128,768]{2,0,1:T(2,128)(2,1)}), bf16[2,128,768]{2,0,1:T(2,128)(2,1)S(1)}, u32[]{:S(2)}, u32[]{:S(2)}) async-start(bf16[2,128,768]{2,0,1:T(2,128)(2,1)} %copy.106), calls=%async_computation.4 | async-start | bytes 786432 | tf_op jit(solution)/shard_map/all_to_all | solution.py:295
  (148 other events, 1712.3 us)
Sparse Core Ops, SparseCore 0:
  9.6 73.1 all-gather.11
  88.4 35.6 all-gather.13
  250.9 224.6 all-gather.23
  477.0 28.6 all-gather.15
  507.1 88.5 all-gather.17
  597.1 87.8 all-gather.19
  701.0 36.8 all-gather.21
  996.5 58.3 reduce-scatter.5
  1057.7 48.0 reduce-scatter.9
  1108.0 160.7 reduce-scatter.11
  1271.2 162.1 reduce-scatter.13
  1435.5 124.3 reduce-scatter.7
  1563.6 122.6 all-reduce.22
where the time goes:
time: 1710 us; the launch traced here: 1700 us
  waiting for transfers between devices  1120 us (65%)
  matrix products  208 us (12%)
  blocking collectives  144 us (8%)
  local copies, waits for them, and re-layouts  119 us (7%)
  other arithmetic  54.6 us (3%)
  starting transfers between devices  38.8 us (2%)
    ppermute x44, waiting for transfers between devices, passed_along(): return lax.ppermute(block, axis, route)  169 us
    reduce_scatter x1, waiting for transfers between devices, body(): lax.psum_scatter(summed[11], 'shard', scatter_dimension=0, tiled=True)  165 us
    all_gather x1, waiting for transfers between devices, combined_all(): gathered = jax.tree.map(lambda a: lax.all_gather(a, axis), part)  164 us
    reduce_scatter x1, waiting for transfers between devices, body(): lax.psum_scatter(summed[9], 'shard', scatter_dimension=0, tiled=True)  163 us
    reduce_scatter x1, waiting for transfers between devices, body(): lax.psum_scatter(summed[2], 'shard', scatter_dimension=0, tiled=True)  127 us
    all_gather x1, waiting for transfers between devices, body(): lax.all_gather(out_weight, 'shard', axis=0, tiled=True)  83.8 us
    psum x1, waiting for transfers between devices, body(): lax.psum((gain_one_grad, shift_one_grad, qkv_grad, query_add_grad, value_...  53.6 us
    dot_general x8, matrix products, backward_step(): jnp.einsum('sqhd,skhd->shqk', grad_block, value_tile, preferred_element_t...  48.2 us
  transfers between devices with their start and end apart: 61, of which 50 were waited for; matrix products, arithmetic and copies ran while one was open for 15% of the time, Pallas kernels for 0%

commit v1 on v0

v1 whole, which is shorter than its diff:
```python
import functools

import jax
import jax.numpy as jnp
from jax import lax
from jax.experimental import pallas as pl
from jax.experimental.pallas import tpu as pltpu
from jax.sharding import PartitionSpec as P

HEADS = 12
HEAD = 64
TILE = 512
EXP2_SCALE = 0.125 * 1.4426950408889634
f32 = jnp.float32
bf16 = jnp.bfloat16
VMEM_LIMIT = 56 * 1024 * 1024


def layer_norm(values, gain, shift):
    centered = values - jnp.mean(values, axis=-1, keepdims=True)
    variance = jnp.mean(centered * centered, axis=-1, keepdims=True)
    return centered * lax.rsqrt(variance + 1e-05) * gain + shift


def gelu_tanh(values):
    return jax.nn.gelu(values, approximate=True)


def swapped(block, bit):
    n = lax.axis_size("ctx")
    return lax.ppermute(block, "ctx", [(i, i ^ (1 << bit)) for i in range(n)])


def mirrored(block):
    n = lax.axis_size("ctx")
    return lax.ppermute(block, "ctx", [(i, n - 1 - i) for i in range(n)])


def shifted(block, distance):
    n = lax.axis_size("shard")
    return lax.ppermute(block, "shard", [(i, (i + distance) % n) for i in range(n)])


def dot(a, b, contract):
    return lax.dot_general(a, b, ((contract[0], contract[1]), ((), ())), preferred_element_type=f32)


def gather_small(block):
    n = lax.axis_size("shard")
    me = lax.axis_index("shard")
    held = jnp.stack([block] + [shifted(block, d) for d in range(1, n)])
    return jnp.take(held, (me - jnp.arange(n)) % n, axis=0)


def reduce_small(parts):
    n = lax.axis_size("shard")
    me = lax.axis_index("shard")
    total = lax.dynamic_index_in_dim(parts, me, 0, False)
    for d in range(1, n):
        total = total + shifted(lax.dynamic_index_in_dim(parts, (me + d) % n, 0, False), d)
    for bit in range(lax.axis_size("ctx").bit_length() - 1):
        total = total + swapped(total, bit)
    return total


def summed_over_chips(part, bits):
    for bit in bits:
        low = part.astype(bf16)
        part = low.astype(f32) + swapped(low, bit).astype(f32)
    return part


def pair_joined(half, odd):
    other = swapped(half, 0)
    return jnp.stack([jnp.where(odd, other, half), jnp.where(odd, half, other)])


def causal_tile(shape):
    return lax.broadcasted_iota(jnp.int32, shape, 0) <= lax.broadcasted_iota(jnp.int32, shape, 1)


def forward_kernel(heads, slots, block, q_ref, kv_ref, att_ref, out_ref, lse_ref, m_ref, l_ref, acc_ref):
    shards, piece, width = q_ref.shape
    rows = shards * piece
    tile = min(TILE, rows)
    per = rows // tile
    queries = q_ref[...].reshape(rows, width)
    for part in range(per):
        first = block[0] * per + part

        def step(j, masked):
            slot = slots[j // per]
            base = pl.multiple_of((j % per) * tile, tile)
            for h in range(heads):
                q = queries[part * tile : (part + 1) * tile, h * HEAD : (h + 1) * HEAD]
                k = kv_ref[slot, pl.ds(base, tile), h * HEAD : (h + 1) * HEAD]
                v = kv_ref[slot, pl.ds(base, tile), width + h * HEAD : width + (h + 1) * HEAD]
                s = dot(k, q, ((1,), (1,))) * EXP2_SCALE
                if masked:
                    s = jnp.where(causal_tile(s.shape), s, -1e30)
                    m = jnp.max(s, axis=0, keepdims=True)
                    p = jnp.exp2(s - m)
                    l_ref[h] = jnp.sum(p, axis=0, keepdims=True)
                    acc_ref[h] = dot(v, p.astype(bf16), ((0,), (0,)))
                else:
                    old = m_ref[h]
                    m = jnp.maximum(old, jnp.max(s, axis=0, keepdims=True))
                    p = jnp.exp2(s - m)
                    factor = jnp.exp2(old - m)
                    l_ref[h] = l_ref[h] * factor + jnp.sum(p, axis=0, keepdims=True)
                    acc_ref[h] = acc_ref[h] * factor + dot(v, p.astype(bf16), ((0,), (0,)))
                m_ref[h] = m

        step(first, True)

        @pl.loop(0, first)
        def _(j):
            step(j, False)

        for h in range(heads):
            total = l_ref[h]
            done = acc_ref[h] / total
            out_ref[h * HEAD : (h + 1) * HEAD, part * tile : (part + 1) * tile] = done
            lse_ref[h, :, part * tile : (part + 1) * tile] = m_ref[h] + jnp.log2(total)
            low = done.astype(bf16)
            for z in range(tile // piece):
                att_ref[part * (tile // piece) + z, h * HEAD : (h + 1) * HEAD, :] = low[
                    :, z * piece : (z + 1) * piece
                ]


def backward_kernel(heads, slots, block, q_ref, kv_ref, go_ref, out_ref, lse_ref, dq_ref, dkv_ref, acc_ref):
    shards, piece, width = q_ref.shape
    rows = shards * piece
    tile = min(TILE, rows)
    per = rows // tile
    blocks = kv_ref.shape[0] * per
    queries = q_ref[...].reshape(rows, width)
    for part in range(per):
        first = block[0] * per + part
        pieces = range(part * (tile // piece), (part + 1) * (tile // piece))
        span = slice(part * tile, (part + 1) * tile)
        go_all = jnp.concatenate([go_ref[z] for z in pieces], axis=1)

        def step(j, masked):
            slot = slots[j // per]
            base = pl.multiple_of((j % per) * tile, tile)
            keys_at = pl.ds(base, tile)
            for h in range(heads):
                lanes = slice(h * HEAD, (h + 1) * HEAD)
                lanes_v = slice(width + h * HEAD, width + (h + 1) * HEAD)
                q = queries[span, lanes]
                go = go_all[lanes]
                delta = jnp.sum(go.astype(f32) * out_ref[lanes, span], axis=0, keepdims=True)
                k = kv_ref[slot, keys_at, lanes]
                v = kv_ref[slot, keys_at, lanes_v]
                p = jnp.exp2(dot(k, q, ((1,), (1,))) * EXP2_SCALE - lse_ref[h, :, span])
                if masked:
                    p = jnp.where(causal_tile(p.shape), p, 0.0)
                pulled = dot(v, go, ((1,), (0,)))
                slopes = (p * (pulled - delta)).astype(bf16)
                dv = dot(p.astype(bf16), go, ((1,), (1,)))
                dk = dot(slopes, q, ((1,), (0,))) * 0.125
                if part:
                    dk = dk + dkv_ref[slot, keys_at, lanes].astype(f32)
                    dv = dv + dkv_ref[slot, keys_at, lanes_v].astype(f32)
                dkv_ref[slot, keys_at, lanes] = dk.astype(bf16)
                dkv_ref[slot, keys_at, lanes_v] = dv.astype(bf16)
                dq = dot(k, slopes, ((0,), (0,)))
                if masked:
                    acc_ref[h] = dq
                else:
                    acc_ref[h] += dq

        if part == 0:

            @pl.loop(first + 1, blocks)
            def _(j):
                base = pl.multiple_of((j % per) * tile, tile)
                dkv_ref[slots[j // per], pl.ds(base, tile), :] = jnp.zeros((tile, 2 * width), bf16)

        elif part:
            pass
        step(first, True)

        @pl.loop(0, first)
        def _(j):
            step(j, False)

        for h in range(heads):
            low = (acc_ref[h] * 0.125).T.astype(bf16)
            for z in pieces:
                at = (z - part * (tile // piece)) * piece
                dq_ref[z, :, h * HEAD : (h + 1) * HEAD] = low[at : at + piece]


def attend(slots, block, queries, kv):
    shards, piece, width = queries.shape
    rows = shards * piece
    heads = width // HEAD
    tile = min(TILE, rows)
    scores = heads * rows * rows * (kv.shape[0] + 1) // 2
    smem = pl.BlockSpec(memory_space=pltpu.SMEM)
    vmem = pl.BlockSpec(memory_space=pltpu.VMEM)
    return pl.pallas_call(
        functools.partial(forward_kernel, heads),
        out_shape=(
            jax.ShapeDtypeStruct((shards, width, piece), bf16),
            jax.ShapeDtypeStruct((width, rows), f32),
            jax.ShapeDtypeStruct((heads, 1, rows), f32),
        ),
        in_specs=[smem, smem, vmem, vmem],
        out_specs=(vmem, vmem, vmem),
        scratch_shapes=[
            pltpu.VMEM((heads, 1, tile), f32),
            pltpu.VMEM((heads, 1, tile), f32),
            pltpu.VMEM((heads, HEAD, tile), f32),
        ],
        compiler_params=pltpu.CompilerParams(vmem_limit_bytes=VMEM_LIMIT),
        cost_estimate=pl.CostEstimate(
            flops=scores * 16 * HEAD, bytes_accessed=2 * kv.size, transcendentals=scores
        ),
        name="attention_forward",
    )(slots, block, queries, kv)


def attend_back(slots, block, queries, kv, grads, out, lse):
    shards, piece, width = queries.shape
    rows = shards * piece
    heads = width // HEAD
    tile = min(TILE, rows)
    scores = heads * rows * rows * (kv.shape[0] + 1) // 2
    smem = pl.BlockSpec(memory_space=pltpu.SMEM)
    vmem = pl.BlockSpec(memory_space=pltpu.VMEM)
    return pl.pallas_call(
        functools.partial(backward_kernel, heads),
        out_shape=(
            jax.ShapeDtypeStruct((shards, piece, width), bf16),
            jax.ShapeDtypeStruct(kv.shape, bf16),
        ),
        in_specs=[smem, smem, vmem, vmem, vmem, vmem, vmem],
        out_specs=(vmem, vmem),
        scratch_shapes=[pltpu.VMEM((heads, HEAD, tile), f32)],
        compiler_params=pltpu.CompilerParams(vmem_limit_bytes=VMEM_LIMIT),
        cost_estimate=pl.CostEstimate(
            flops=scores * 40 * HEAD, bytes_accessed=4 * kv.size, transcendentals=scores
        ),
        name="attention_backward",
    )(slots, block, queries, kv, grads, out, lse)


def body(
    layer_input,
    attn_gain,
    attn_shift,
    qkv_weight,
    query_bias,
    value_bias,
    proj_weight,
    proj_bias,
    mlp_gain,
    mlp_shift,
    fc_weight,
    fc_bias,
    out_weight,
    out_bias,
    grad_output,
):
    seqs, piece, width = layer_input.shape
    cycle = lax.axis_size("ctx")
    shards = lax.axis_size("shard")
    here = lax.axis_index("ctx")
    shard_at = lax.axis_index("shard")
    odd = here % 2
    bits = cycle.bit_length() - 1
    chip_bits = list(range(1, bits))
    orders = (chip_bits + [0], chip_bits[::-1] + [0])
    rows = shards * piece
    local_width = qkv_weight.shape[0]
    local_hidden = out_weight.shape[0]
    half_hidden = local_hidden // 2
    heads = -(-HEADS // shards)
    group = heads * HEAD
    padded = group * shards
    straight = (seqs + 1) // 2

    def mirror_late(rows_held):
        return jnp.concatenate([rows_held[:straight], mirrored(rows_held[straight:])])

    inputs = mirror_late(layer_input)
    grads = mirror_late(grad_output)
    gathered_inputs = lax.all_gather(inputs, "shard", axis=0)

    packed = jnp.concatenate(
        [
            jnp.stack(
                [attn_gain, attn_shift, query_bias, value_bias, proj_bias, mlp_gain, mlp_shift, out_bias]
            ),
            fc_bias.reshape(-1, local_width),
        ]
    )
    small = gather_small(packed).astype(f32)
    vectors = [small[:, i].reshape(-1) for i in range(8)]
    gain_one, shift_one, query_add, value_add, proj_add, gain_two, shift_two, out_add = vectors
    fc_add = lax.dynamic_index_in_dim(
        small[:, 8:].reshape(shards, 2, half_hidden), odd, 1, False
    ).reshape(-1)

    def own_heads(vector):
        return lax.dynamic_slice_in_dim(
            jnp.pad(vector, (0, padded - width)), shard_at * group, group, 0
        )

    def by_heads(weight):
        parts = jnp.pad(
            weight.reshape(local_width, 3, width), ((0, 0), (0, 0), (0, padded - width))
        ).reshape(local_width, 3, shards, group)
        return parts.transpose(2, 0, 1, 3).reshape(shards, local_width, 3 * group)

    qkv_own = lax.all_to_all(by_heads(qkv_weight), "shard", 0, 0, tiled=True).reshape(
        width, 3 * group
    )
    q_weight = qkv_own[:, :group]
    kv_weight = qkv_own[:, group:]

    proj_full = lax.all_gather(proj_weight, "shard", axis=0, tiled=True)
    fc_half = lax.all_gather(
        lax.dynamic_index_in_dim(
            fc_weight.reshape(local_width, shards, 2, half_hidden), odd, 2, False
        ).reshape(local_width, shards * half_hidden),
        "shard",
        axis=0,
        tiled=True,
    )
    out_half = lax.all_gather(
        lax.dynamic_index_in_dim(out_weight.reshape(2, half_hidden, width), odd, 0, False),
        "shard",
        axis=0,
        tiled=True,
    )

    normed_one = layer_norm(gathered_inputs.astype(f32), gain_one, shift_one).astype(bf16)
    queries = (dot(normed_one, q_weight, ((3,), (0,))) + own_heads(query_add)).astype(bf16)
    kv_add = jnp.concatenate([jnp.zeros((group,), f32), own_heads(value_add)])
    kv_own = (dot(normed_one, kv_weight, ((3,), (0,))) + kv_add).astype(bf16)

    attended_parts = []
    saved = []
    for seq in range(seqs):
        order = orders[seq % 2]
        late = seq >= straight
        held = kv_own[:, seq].reshape(1, rows, 2 * group)
        for bit in order:
            held = jnp.concatenate([held, swapped(held, bit)])
        owners = jnp.arange(cycle)
        if late:
            owners = cycle - 1 - owners
        apart = owners ^ here
        slots = sum(((apart >> bit) & 1) << k for k, bit in enumerate(order)).astype(jnp.int32)
        block = (cycle - 1 - here if late else here).astype(jnp.int32).reshape(1)
        att, out, lse = attend(slots, block, queries[:, seq], held)
        attended_parts.append(att)
        saved.append((order, slots, block, held, out, lse))
    attended = lax.all_to_all(
        jnp.concatenate(attended_parts, axis=2), "shard", 0, 0, tiled=True
    ).reshape(padded, seqs * piece)[:width]

    inputs32 = inputs.astype(f32).reshape(seqs * piece, width)
    grads_own = grads.reshape(seqs * piece, width)
    grads32 = grads_own.astype(f32)
    middle = inputs32 + dot(attended, proj_full, ((0,), (0,))) + proj_add
    normed_two = layer_norm(middle, gain_two, shift_two).astype(bf16)

    normed_pair = jnp.stack([normed_two, swapped(normed_two, 0)])
    grads_pair = jnp.stack([grads_own, swapped(grads_own, 0)])
    preactivation = dot(normed_pair, fc_half, ((2,), (0,))) + fc_add
    hidden = gelu_tanh(preactivation).astype(bf16)
    out_part = dot(hidden, out_half, ((2,), (0,)))
    layer_output = (middle + (out_part[0] + swapped(out_part[1], 0)) + out_add).astype(bf16)
    grad_hidden = dot(grads_pair, out_half, ((2,), (1,)))
    grad_pre = jax.vjp(gelu_tanh, preactivation)[1](grad_hidden)[0].astype(bf16)
    normed_part = dot(grad_pre, fc_half, ((2,), (1,)))
    grad_normed_two = normed_part[0] + swapped(normed_part[1], 0)
    grad_mid_part, gain_two_grad, shift_two_grad = jax.vjp(
        layer_norm, middle, gain_two, shift_two
    )[1](grad_normed_two)
    grad_middle = grads32 + grad_mid_part
    grad_branch = grad_middle.astype(bf16)

    grad_attended = jnp.pad(
        dot(proj_full, grad_branch, ((1,), (1,))).astype(bf16), ((0, padded - width), (0, 0))
    ).reshape(shards, group, seqs * piece)
    grad_heads = lax.all_to_all(grad_attended, "shard", 0, 0, tiled=True)
    query_grads = []
    kv_grads = []
    for seq in range(seqs):
        order, slots, block, held, out, lse = saved[seq]
        dq, dkv = attend_back(
            slots,
            block,
            queries[:, seq],
            held,
            grad_heads[:, :, seq * piece : (seq + 1) * piece],
            out,
            lse,
        )
        query_grads.append(dq)
        for bit in order[::-1]:
            split = dkv.shape[0] // 2
            received = swapped(dkv[split:], bit)
            dkv = (dkv[:split].astype(f32) + received.astype(f32)).astype(bf16)
        kv_grads.append(dkv.reshape(shards, piece, 2 * group))
    query_low = jnp.stack(query_grads, axis=1)
    kv_low = jnp.stack(kv_grads, axis=1)

    normed_part_one = dot(query_low, q_weight, ((3,), (1,))) + dot(kv_low, kv_weight, ((3,), (1,)))
    grad_normed_one = lax.psum_scatter(
        normed_part_one.astype(bf16), "shard", scatter_dimension=0, tiled=False
    ).astype(f32).reshape(seqs * piece, width)
    grad_in_part, gain_one_grad, shift_one_grad = jax.vjp(
        layer_norm, inputs32, gain_one, shift_one
    )[1](grad_normed_one)
    input_grad = (grad_middle + grad_in_part).astype(bf16)
    layer_output = mirror_late(layer_output.reshape(seqs, piece, width))
    input_grad = mirror_late(input_grad.reshape(seqs, piece, width))

    def pair_split(grad):
        parts = grad.astype(bf16).reshape(shards, 2, local_width // 2, -1)
        mine = lax.dynamic_index_in_dim(parts, odd, 1, False)
        sent = lax.dynamic_index_in_dim(parts, 1 - odd, 1, False)
        return (mine.astype(f32) + swapped(sent, 0).astype(f32)).astype(bf16)

    flat_tokens = ((0, 1), (0, 1))
    out_grad = dot(hidden, grads_pair, flat_tokens).astype(bf16)
    out_grad = lax.psum_scatter(
        out_grad.reshape(shards, half_hidden, width), "shard", scatter_dimension=0, tiled=False
    )
    out_grad = pair_joined(summed_over_chips(out_grad, chip_bits[::-1]), odd).reshape(
        local_hidden, width
    )
    fc_grad = dot(normed_pair, grad_pre, flat_tokens).astype(bf16)
    fc_grad = lax.psum_scatter(
        fc_grad.reshape(shards, local_width, -1), "shard", scatter_dimension=0, tiled=False
    )
    fc_grad = pair_joined(summed_over_chips(fc_grad, chip_bits), odd)
    fc_grad = (
        fc_grad.reshape(2, local_width, shards, half_hidden)
        .transpose(1, 2, 0, 3)
        .reshape(local_width, shards * local_hidden)
    )
    proj_grad = lax.psum_scatter(
        pair_split(dot(attended, grad_branch, ((1,), (0,)))), "shard", scatter_dimension=0, tiled=False
    )
    proj_grad = pair_joined(summed_over_chips(proj_grad, chip_bits), odd).reshape(local_width, width)
    tokens3 = ((0, 1, 2), (0, 1, 2))
    qkv_grad = jnp.concatenate(
        [dot(normed_one, query_low, tokens3), dot(normed_one, kv_low, tokens3)], axis=1
    )
    qkv_grad = lax.all_to_all(pair_split(qkv_grad), "shard", 0, 0, tiled=True)
    qkv_grad = pair_joined(summed_over_chips(qkv_grad, chip_bits), odd)
    qkv_grad = (
        qkv_grad.reshape(2, shards, local_width // 2, 3, group)
        .transpose(0, 2, 3, 1, 4)
        .reshape(local_width, 3, padded)[:, :, :width]
        .reshape(local_width, 3 * width)
    )

    fc_add_part = jnp.sum(grad_pre.astype(f32), axis=(0, 1)).reshape(shards, 1, half_hidden)
    fc_add_part = jnp.where(jnp.arange(2)[None, :, None] == odd, fc_add_part, 0.0)
    early = reduce_small(
        jnp.concatenate(
            [
                v.reshape(shards, -1)
                for v in (
                    gain_two_grad,
                    shift_two_grad,
                    jnp.sum(grad_branch.astype(f32), axis=0),
                    jnp.sum(grads32, axis=0),
                    fc_add_part,
                )
            ],
            axis=1,
        )
    )

    def all_heads(vector):
        return lax.dynamic_update_slice_in_dim(
            jnp.zeros((padded,), f32), vector, shard_at * group, 0
        )[:width]

    late_sums = reduce_small(
        jnp.concatenate(
            [
                v.reshape(shards, -1)
                for v in (
                    gain_one_grad,
                    shift_one_grad,
                    all_heads(jnp.sum(query_low.astype(f32), axis=(0, 1, 2))),
                    all_heads(jnp.sum(kv_low[..., group:].astype(f32), axis=(0, 1, 2))),
                )
            ],
            axis=1,
        )
    )
    early_parts = [early[i * local_width : (i + 1) * local_width] for i in range(4)]
    late_parts = [late_sums[i * local_width : (i + 1) * local_width] for i in range(4)]
    return (
        layer_output,
        input_grad,
        late_parts[0],
        late_parts[1],
        qkv_grad,
        late_parts[2],
        late_parts[3],
        proj_grad,
        early_parts[2],
        early_parts[0],
        early_parts[1],
        fc_grad,
        early[4 * local_width :],
        out_grad,
        early_parts[3],
    )


def solution(mesh):
    tokens = P(None, ("ctx", "shard"), None)
    vector = P("shard")
    matrix = P("shard", None)
    return jax.shard_map(
        body,
        mesh=mesh,
        in_specs=(
            tokens,
            vector,
            vector,
            matrix,
            vector,
            vector,
            matrix,
            vector,
            vector,
            vector,
            matrix,
            vector,
            matrix,
            vector,
            tokens,
        ),
        out_specs=(
            tokens,
            tokens,
            vector,
            vector,
            matrix,
            vector,
            vector,
            matrix,
            vector,
            vector,
            vector,
            matrix,
            vector,
            matrix,
            vector,
        ),
        check_vma=False,
    )
```

time: 1710 us -> 486 us (0.28)
  waiting for transfers between devices: 1120 us -> 180 us
  matrix products: 208 us -> 41.6 us
  blocking collectives: 144 us -> 0 us
  local copies, waits for them, and re-layouts: 119 us -> 67.7 us
  Pallas kernels: 0 us -> 47.9 us
  starting transfers between devices: 38.8 us -> 67.5 us
    reduce_scatter x5 -> x4, waiting for transfers between devices: 524 us -> 0.03 us  [the longest x1 0.02 us: body(): lax.psum_scatter(normed_part_one.astype(bf16), 'shard', scatter_dimension...]
    all_gather x7 -> x4, waiting for transfers between devices: 361 us -> 63.8 us  [the longest x1 32 us: body(): gathered_inputs = lax.all_gather(inputs, 'shard', axis=0)]
    dot_general x67 -> x15, matrix products: 208 us -> 41.6 us  [dot(): lax.dot_general(a, b, ((contract[0], contract[1]), ((), ())), preferred_e...]
    ppermute x44 -> x49, waiting for transfers between devices: 169 us -> 84.6 us  [the longest x36 67.3 us: swapped(): return lax.ppermute(block, 'ctx', [(i, i ^ 1 << bit) for i in range(n)])]
    all_gather x5 -> x0, blocking collectives: 82.1 us -> none  [the longest x2 40.8 us: combined_all(): gathered = jax.tree.map(lambda a: lax.all_gather(a, axis), part)]
    psum x1 -> x0, waiting for transfers between devices: 53.6 us -> none  [body(): lax.psum((gain_one_grad, shift_one_grad, qkv_grad, query_add_grad, value_...]
    pallas_call x0 -> x4, Pallas kernels: none -> 47.9 us  [the longest x2 27.5 us: attend_back(): pl.pallas_call(functools.partial(backward_kernel, heads), out_shape=(jax....]
    while x163 -> x0, local copies, waits for them, and re-layouts: 42.4 us -> none
  transfers between devices with their start and end apart: 61 -> 61, of which waited for: 50 -> 25; matrix products, arithmetic and copies ran while one was open for 15% -> 29% of each run, Pallas kernels for 0% -> 10%
where the time goes in v1:
time: 486 us; the launch traced here: 478 us
  waiting for transfers between devices  180 us (37%)
  local copies, waits for them, and re-layouts  67.7 us (14%)
  starting transfers between devices  67.5 us (14%)
  other arithmetic  57.4 us (12%)
  Pallas kernels  47.9 us (10%)
  matrix products  41.6 us (9%)
  between operations  15.9 us (3%)
    ppermute x36, waiting for transfers between devices, swapped(): return lax.ppermute(block, 'ctx', [(i, i ^ 1 << bit) for i in range(n)])  67.3 us
    dot_general x15, matrix products, dot(): lax.dot_general(a, b, ((contract[0], contract[1]), ((), ())), preferred_e...  41.6 us
    all_gather x1, waiting for transfers between devices, body(): gathered_inputs = lax.all_gather(inputs, 'shard', axis=0)  32 us
    all_gather x1, waiting for transfers between devices, body(): lax.all_gather(lax.dynamic_index_in_dim(out_weight.reshape(2, half_hidden...  31.9 us
    ppermute x36, starting transfers between devices, swapped(): return lax.ppermute(block, 'ctx', [(i, i ^ 1 << bit) for i in range(n)])  29.9 us
    pallas_call x2, Pallas kernels, attend_back(): pl.pallas_call(functools.partial(backward_kernel, heads), out_shape=(jax....  27.5 us
    pallas_call x2, Pallas kernels, attend(): pl.pallas_call(functools.partial(forward_kernel, heads), out_shape=(jax.S...  20.4 us
    all_to_all x1, waiting for transfers between devices, body(): grad_heads = lax.all_to_all(grad_attended, 'shard', 0, 0, tiled=True)  15.5 us
  transfers between devices with their start and end apart: 61, of which 25 were waited for; matrix products, arithmetic and copies ran while one was open for 29% of the time, Pallas kernels for 10%

profile of v1, /device:TPU:0, one launch (start us, length us, event | category | flops | bytes accessed | tf_op | source)
XLA Modules:
  0.0 477.9 jit_solution(16843489145076928193)
XLA Ops:
  12.6 5.3 %collective-permute-done = bf16[1,128,768]{2,1,0:T(8,128)(2,1)S(1)} collective-permute-done((bf16[1,128,768]{2,1,0:T(8,128)(2,1)S(1)}, bf16[1,128,768]{2,1,0:T(8,128)(2,1)S(1)}, u32[]{:S(2)}, u32[]{:S(2)}) %collective-permute-start) | collective-permute-done | bytes 196640 | tf_op jit(solution)/shard_map/ppermute | solution.py:36
  20.1 4.5 collective-permute-start.3
  31.6 4.2 all-to-all-start
  46.6 32.0 %all-gather.11.cloned.1.call-done = bf16[8,128,768]{2,1,0:T(8,128)(2,1)} async-done(((bf16[2,128,768]{2,1,0:T(8,128)(2,1)}), bf16[8,128,768]{2,1,0:T(8,128)(2,1)}) %all-gather.11.cloned.1.call-update) | async-done | bytes 1572880 | tf_op jit(solution)/shard_map/all_gather | solution.py:292
  91.9 7.5 %collective-permute-done.7 = bf16[1,512,384]{2,1,0:T(8,128)(2,1)S(1)} collective-permute-done((bf16[1,512,384]{2,1,0:T(8,128)(2,1)S(1)}, bf16[1,512,384]{2,1,0:T(8,128)(2,1)S(1)}, u32[]{:S(2)}, u32[]{:S(2)}) %collective-permute-start.7) | collective-permute-done | bytes 393248 | tf_op jit(solution)/shard_map/ppermute | solution.py:31
  102.6 15.0 %collective-permute-done.8 = bf16[2,512,384]{2,1,0:T(8,128)(2,1)S(1)} collective-permute-done((bf16[2,512,384]{2,1,0:T(8,128)(2,1)S(1)}, bf16[2,512,384]{2,1,0:T(8,128)(2,1)S(1)}, u32[]{:S(2)}, u32[]{:S(2)}) %collective-permute-start.8) | collective-permute-done | bytes 786464 | tf_op jit(solution)/shard_map/ppermute | solution.py:31
  132.2 16.2 %attention_forward.3 = (bf16[4,192,128]{2,1,0:T(8,128)(2,1)}, f32[192,512]{1,0:T(8,128)}, f32[3,1,512]{2,1,0:T(1,128)}) custom-call(s32[8]{0:T(128)} %shift-left_add_fusion.slots, s32[1]{0:T(128)} %bitcast.17.block, bf16[4,128,192]{2,1,0:T(8,128)(2,1)} %get-tuple-element.75.q_ref, bf16[8,512,384]{2,1,0:T(8,128)(2,1)} %pad_maximum_fusion.1.kv_ref), custom_call_target="tpu_custom_call" | custom-call | flops 3623878656 | bytes 3145728 | tf_op jit(solution)/shard_map/attention_forward/pallas_call | solution.py:205
  148.4 4.2 attention_forward.2
  160.5 9.4 %all-to-all-done.1 = bf16[4,192,256]{2,1,0:T(8,128)(2,1)S(1)} async-done(((bf16[4,192,256]{2,1,0:T(8,128)(2,1)}), bf16[4,192,256]{2,1,0:T(8,128)(2,1)S(1)}, u32[]{:S(2)}, u32[]{:S(2)}) %all-to-all-start.1) | async-done | bytes 393248 | tf_op jit(solution)/shard_map/all_to_all | solution.py:364
  174.5 4.9 %convolution_add_fusion = f32[2,256,1536]{2,1,0:T(8,128)} fusion(bf16[768,1536]{1,0:T(8,128)(2,1)} %all-gather.9.cloned.1.call-done, f32[1536]{0:T(1024)S(1)} %add.368, bf16[1,256,768]{2,1,0:T(8,128)(2,1)} %bitcast.22, bf16[1,256,768]{2,1,0:T(8,128)(2,1)S(1)} %fusion.92), kind=kOutput, calls=%fused_computation.5 | convolution fusion | flops 1209139200 | bytes 6297600 | tf_op jit(solution)/shard_map/dot_general | solution.py:45
  179.4 31.9 %all-gather.13.cloned.1.call-done = bf16[1,1536,768]{2,1,0:T(8,128)(2,1)} async-done(((bf16[1,384,768]{2,1,0:T(8,128)(2,1)}), bf16[1,1536,768]{2,1,0:T(8,128)(2,1)}) %all-gather.13.cloned.1.call-update) | async-done | bytes 2359312 | tf_op jit(solution)/shard_map/all_gather | solution.py:335
  211.3 6.5 %convert_reduce_fusion = (f32[1536]{0:T(1024)}, bf16[2,256,1536]{2,1,0:T(8,128)(2,1)S(1)}) fusion(f32[2,256,1536]{2,1,0:T(8,128)} %convolution_add_fusion, bf16[1,1536,768]{2,1,0:T(8,128)(2,1)} %all-gather.13.cloned.1.call-done, bf16[1,256,768]{2,1,0:T(8,128)(2,1)} %bitcast.33, bf16[1,256,768]{2,1,0:T(8,128)(2,1)S(1)} %bitcast.232), kind=kOutput, calls=%fused_computation.15 | convolution fusion | flops 1225652736 | bytes 7870464 | tf_op jit(solution)/shard_map/dot_general | solution.py:45
  235.5 4.4 bitcast_convert_fusion.1
  246.3 15.5 %all-to-all-done.2 = bf16[4,192,256]{2,1,0:T(8,128)(2,1)S(1)} async-done(((bf16[4,192,256]{2,1,0:T(8,128)(2,1)}), bf16[4,192,256]{2,1,0:T(8,128)(2,1)S(1)}, u32[]{:S(2)}, u32[]{:S(2)}) %all-to-all-start.2) | async-done | bytes 393248 | tf_op jit(solution)/shard_map/all_to_all | solution.py:393
  262.6 6.7 %attention_backward.2 = (bf16[4,128,192]{2,1,0:T(8,128)(2,1)}, bf16[8,512,384]{2,1,0:T(8,128)(2,1)}) custom-call(s32[8]{0:T(128)} %shift-left_add_fusion.1.slots, s32[1]{0:T(128)} %bitcast.1.block, bf16[4,128,192]{2,1,0:T(8,128)(2,1)} %get-tuple-element.74.q_ref, bf16[8,512,384]{2,1,0:T(8,128)(2,1)} %pad_maximum_fusion.kv_ref, ...), custom_call_target="tpu_custom_call" | custom-call | flops 9059696640 | bytes 6291456 | tf_op jit(solution)/shard_map/attention_backward/pallas_call | solution.py:235
  274.2 20.8 %attention_backward.3 = (bf16[4,128,192]{2,1,0:T(8,128)(2,1)}, bf16[8,512,384]{2,1,0:T(8,128)(2,1)}) custom-call(s32[8]{0:T(128)} %shift-left_add_fusion.slots, s32[1]{0:T(128)} %bitcast.17.block, bf16[4,128,192]{2,1,0:T(8,128)(2,1)} %get-tuple-element.75.q_ref, bf16[8,512,384]{2,1,0:T(8,128)(2,1)} %pad_maximum_fusion.1.kv_ref, ...), custom_call_target="tpu_custom_call" | custom-call | flops 9059696640 | bytes 6291456 | tf_op jit(solution)/shard_map/attention_backward/pallas_call | solution.py:235
  298.6 5.2 %bitcast_convert_fusion = bf16[1536,768]{1,0:T(8,128)(2,1)} fusion(bf16[1,256,768]{2,1,0:T(8,128)(2,1)} %bitcast.33, bf16[1,256,768]{2,1,0:T(8,128)(2,1)S(1)} %bitcast.233, f32[2,256,1536]{2,1,0:T(8,128)} %convolution_add_fusion), kind=kOutput, calls=%fused_computation.1 | convolution fusion | flops 1216610304 | bytes 6291456 | tf_op jit(solution)/shard_map/dot_general | solution.py:45
  305.0 4.0 collective-permute-start.39
  318.8 15.4 %collective-permute-done.41 = f32[1536]{0:T(1024)S(1)} collective-permute-done((f32[1536]{0:T(1024)S(1)}, f32[1536]{0:T(1024)S(1)}, u32[]{:S(2)}, u32[]{:S(2)}) %collective-permute-start.41) | collective-permute-done | bytes 6176 | tf_op jit(solution)/shard_map/ppermute | solution.py:31
  373.3 5.6 %all-to-all-done.3 = bf16[4,96,576]{2,1,0:T(8,128)(2,1)S(1)} async-done(((bf16[4,96,576]{2,1,0:T(8,128)(2,1)}), bf16[4,96,576]{2,1,0:T(8,128)(2,1)S(1)}, u32[]{:S(2)}, u32[]{:S(2)}) %all-to-all-start.3) | async-done | bytes 442400 | tf_op jit(solution)/shard_map/all_to_all | solution.py:459
  383.2 8.2 %collective-permute-done.30 = bf16[4,96,576]{2,1,0:T(8,128)(2,1)} collective-permute-done((bf16[4,96,576]{2,1,0:T(8,128)(2,1)S(1)}, bf16[4,96,576]{2,1,0:T(8,128)(2,1)}, u32[]{:S(2)}, u32[]{:S(2)}) %collective-permute-start.30) | collective-permute-done | bytes 442400 | tf_op jit(solution)/shard_map/ppermute | solution.py:31
  394.7 4.4 add_convert_fusion
  402.1 8.9 %collective-permute-done.31 = bf16[4,96,576]{2,1,0:T(8,128)(2,1)S(1)} collective-permute-done((bf16[4,96,576]{2,1,0:T(8,128)(2,1)S(1)}, bf16[4,96,576]{2,1,0:T(8,128)(2,1)S(1)}, u32[]{:S(2)}, u32[]{:S(2)}) %collective-permute-start.31) | collective-permute-done | bytes 442400 | tf_op jit(solution)/shard_map/ppermute | solution.py:31
  465.3 4.5 collective-permute-done.22
  (449 shorter events, 216.7 us)
Async XLA Ops:
  7.3 71.3 %all-gather.11.cloned.1.call-start = ((), (), s32[]{:S(2)}) async-start(), calls=%async_computation.14 | async-start | bytes 1966080 | tf_op jit(solution)/shard_map/all_gather | solution.py:292
  19.0 141.5 %all-gather.7.cloned.1.call-start = ((), (), s32[]{:S(2)}) async-start(), calls=%async_computation.8 | async-start | bytes 1474560 | tf_op jit(solution)/shard_map/all_gather | solution.py:326
  20.1 24.2 %collective-permute-start.3 = (bf16[12,192]{1,0:T(8,128)(2,1)S(1)}, bf16[12,192]{1,0:T(8,128)(2,1)S(1)}, u32[]{:S(2)}, u32[]{:S(2)}) collective-permute-start(bf16[12,192]{1,0:T(8,128)(2,1)S(1)} %concatenate.72), channel_id=1, source_target_pairs={{0,3},{1,0},{2,1},{3,2},{4,7},{5,4},{6,5},{7,6},{8,11},{9,8},{10,9... | collective-permute-start | bytes 13832 | tf_op jit(solution)/shard_map/ppermute | solution.py:41
  24.5 19.7 %collective-permute-start.2 = (bf16[12,192]{1,0:T(8,128)(2,1)S(1)}, bf16[12,192]{1,0:T(8,128)(2,1)S(1)}, u32[]{:S(2)}, u32[]{:S(2)}) collective-permute-start(bf16[12,192]{1,0:T(8,128)(2,1)S(1)} %concatenate.72), channel_id=1, source_target_pairs={{0,2},{1,3},{2,0},{3,1},{4,6},{5,7},{6,4},{7,5},{8,10},{9,11},{10,... | collective-permute-start | bytes 13832 | tf_op jit(solution)/shard_map/ppermute | solution.py:41
  24.5 19.7 %collective-permute-start.1 = (bf16[12,192]{1,0:T(8,128)(2,1)S(1)}, bf16[12,192]{1,0:T(8,128)(2,1)S(1)}, u32[]{:S(2)}, u32[]{:S(2)}) collective-permute-start(bf16[12,192]{1,0:T(8,128)(2,1)S(1)} %concatenate.72), channel_id=1, source_target_pairs={{0,1},{1,2},{2,3},{3,0},{4,5},{5,6},{6,7},{7,4},{8,9},{9,10},{10,1... | collective-permute-start | bytes 13832 | tf_op jit(solution)/shard_map/ppermute | solution.py:41
  31.6 53.9 %all-to-all-start = ((bf16[4,192,576]{2,1,0:T(8,128)(2,1)}), bf16[4,192,576]{2,1,0:T(8,128)(2,1)}, u32[]{:S(2)}, u32[]{:S(2)}) async-start(bf16[4,192,576]{2,1,0:T(8,128)(2,1)} %copy.93), calls=%async_computation | async-start | bytes 1966080 | tf_op jit(solution)/shard_map/all_to_all | solution.py:320
  35.8 138.6 %all-gather.9.cloned.1.call-start = ((), (), s32[]{:S(2)}) async-start(), calls=%async_computation.9 | async-start | bytes 2949120 | tf_op jit(solution)/shard_map/all_gather | solution.py:327
  43.9 167.4 %all-gather.13.cloned.1.call-start = ((), (), s32[]{:S(2)}) async-start(), calls=%async_computation.15 | async-start | bytes 2949120 | tf_op jit(solution)/shard_map/all_gather | solution.py:335
  99.5 18.1 %collective-permute-start.8 = (bf16[2,512,384]{2,1,0:T(8,128)(2,1)S(1)}, bf16[2,512,384]{2,1,0:T(8,128)(2,1)S(1)}, u32[]{:S(2)}, u32[]{:S(2)}) collective-permute-start(bf16[2,512,384]{2,1,0:T(8,128)(2,1)S(1)} %pad_maximum_fusion.6), channel_id=1, source_target_pairs={{0,8},{4,12},{8,0},{12,4},{16,24},{20,28},{24,16},{28,20},{1,9},{5... | collective-permute-start | bytes 2359304 | tf_op jit(solution)/shard_map/ppermute | solution.py:31
  101.1 17.9 %collective-permute-start.5 = (bf16[2,512,384]{2,1,0:T(8,128)(2,1)S(1)}, bf16[2,512,384]{2,1,0:T(8,128)(2,1)S(1)}, u32[]{:S(2)}, u32[]{:S(2)}) collective-permute-start(bf16[2,512,384]{2,1,0:T(8,128)(2,1)S(1)} %pad_maximum_fusion.5), channel_id=1, source_target_pairs={{0,16},{4,20},{8,24},{12,28},{16,0},{20,4},{24,8},{28,12},{1,17},{... | collective-permute-start | bytes 2359304 | tf_op jit(solution)/shard_map/ppermute | solution.py:31
  157.9 200.7 %reduce-scatter.7.cloned.1.call-start = ((), (), s32[]{:S(2)}) async-start(), calls=%async_computation.11 | async-start | bytes 737280 | tf_op jit(solution)/shard_map/reduce_scatter | solution.py:451
  235.5 129.2 %reduce-scatter.9.cloned.1.call-start = ((), (), s32[]{:S(2)}) async-start(), calls=%async_computation.12 | async-start | bytes 2949120 | tf_op jit(solution)/shard_map/reduce_scatter | solution.py:442
  242.6 19.2 %all-to-all-start.2 = ((bf16[4,192,256]{2,1,0:T(8,128)(2,1)}), bf16[4,192,256]{2,1,0:T(8,128)(2,1)S(1)}, u32[]{:S(2)}, u32[]{:S(2)}) async-start(bf16[4,192,256]{2,1,0:T(8,128)(2,1)} %bitcast.37), calls=%async_computation.2 | async-start | bytes 786432 | tf_op jit(solution)/shard_map/all_to_all | solution.py:393
  246.1 125.8 %reduce-scatter.11.cloned.1.call-start = ((), (), s32[]{:S(2)}) async-start(), calls=%async_computation.13 | async-start | bytes 2949120 | tf_op jit(solution)/shard_map/reduce_scatter | solution.py:435
  272.0 36.9 %collective-permute-start.16 = (bf16[4,512,384]{2,1,0:T(8,128)(2,1)}, bf16[4,512,384]{2,1,0:T(8,128)(2,1)}, u32[]{:S(2)}, u32[]{:S(2)}) collective-permute-start(bf16[4,512,384]{2,1,0:T(8,128)(2,1)} %slice.197), channel_id=1, source_target_pairs={{0,4},{4,0},{8,12},{12,8},{16,20},{20,16},{24,28},{28,24},{1,5},{5... | collective-permute-start | bytes 4718600 | tf_op jit(solution)/shard_map/ppermute | solution.py:31
  311.5 23.4 %collective-permute-start.17 = (bf16[2,512,384]{2,1,0:T(8,128)(2,1)S(1)}, bf16[2,512,384]{2,1,0:T(8,128)(2,1)S(1)}, u32[]{:S(2)}, u32[]{:S(2)}) collective-permute-start(bf16[2,512,384]{2,1,0:T(8,128)(2,1)S(1)} %slice.248), channel_id=1, source_target_pairs={{0,16},{4,20},{8,24},{12,28},{16,0},{20,4},{24,8},{28,12},{1,17},{... | collective-permute-start | bytes 2359304 | tf_op jit(solution)/shard_map/ppermute | solution.py:31
  314.9 22.5 %collective-permute-start.20 = (bf16[2,512,384]{2,1,0:T(8,128)(2,1)S(1)}, bf16[2,512,384]{2,1,0:T(8,128)(2,1)S(1)}, u32[]{:S(2)}, u32[]{:S(2)}) collective-permute-start(bf16[2,512,384]{2,1,0:T(8,128)(2,1)S(1)} %slice.252), channel_id=1, source_target_pairs={{0,8},{4,12},{8,0},{12,4},{16,24},{20,28},{24,16},{28,20},{1,9},{5... | collective-permute-start | bytes 2359304 | tf_op jit(solution)/shard_map/ppermute | solution.py:31
  334.3 18.5 %collective-permute-start.42 = (f32[1536]{0:T(1024)S(1)}, f32[1536]{0:T(1024)S(1)}, u32[]{:S(2)}, u32[]{:S(2)}) collective-permute-start(f32[1536]{0:T(1024)S(1)} %add.417), channel_id=1, source_target_pairs={{0,16},{4,20},{8,24},{12,28},{16,0},{20,4},{24,8},{28,12},{1,17},{... | collective-permute-start | bytes 18440 | tf_op jit(solution)/shard_map/ppermute | solution.py:31
  361.1 17.9 %all-to-all-start.3 = ((bf16[4,96,576]{2,1,0:T(8,128)(2,1)}), bf16[4,96,576]{2,1,0:T(8,128)(2,1)S(1)}, u32[]{:S(2)}, u32[]{:S(2)}) async-start(bf16[4,96,576]{2,1,0:T(8,128)(2,1)} %fusion.26), calls=%async_computation.4 | async-start | bytes 983040 | tf_op jit(solution)/shard_map/all_to_all | solution.py:459
  364.6 80.0 %reduce-scatter.5.cloned.1.call-start = ((), (), s32[]{:S(2)}) async-start(), calls=%async_computation.10 | async-start | bytes 1966080 | tf_op jit(solution)/shard_map/reduce_scatter | solution.py:417
  371.8 43.7 %collective-permute-start.36 = (f32[96,768]{1,0:T(8,128)}, f32[96,768]{1,0:T(8,128)}, u32[]{:S(2)}, u32[]{:S(2)}) collective-permute-start(f32[96,768]{1,0:T(8,128)} %convert_add_fusion.5), channel_id=1, source_target_pairs={{0,4},{4,0},{8,12},{12,8},{16,20},{20,16},{24,28},{28,24},{1,5},{5... | collective-permute-start | bytes 884744 | tf_op jit(solution)/shard_map/ppermute | solution.py:31
  371.8 27.3 %collective-permute-start.46 = (bf16[384,768]{1,0:T(8,128)(2,1)}, bf16[384,768]{1,0:T(8,128)(2,1)}, u32[]{:S(2)}, u32[]{:S(2)}) collective-permute-start(bf16[384,768]{1,0:T(8,128)(2,1)} %bitcast.251), channel_id=1, source_target_pairs={{0,16},{4,20},{8,24},{12,28},{16,0},{20,4},{24,8},{28,12},{1,17},{... | collective-permute-start | bytes 1769480 | tf_op jit(solution)/shard_map/ppermute | solution.py:31
  381.6 31.1 %collective-permute-start.44 = (bf16[192,1536]{1,0:T(8,128)(2,1)S(1)}, bf16[192,1536]{1,0:T(8,128)(2,1)}, u32[]{:S(2)}, u32[]{:S(2)}) collective-permute-start(bf16[192,1536]{1,0:T(8,128)(2,1)S(1)} %add_convert_fusion.8), channel_id=1, source_target_pairs={{0,16},{4,20},{8,24},{12,28},{16,0},{20,4},{24,8},{28,12},{1,17},{... | collective-permute-start | bytes 1769480 | tf_op jit(solution)/shard_map/ppermute | solution.py:31
  420.8 20.6 %collective-permute-start.48 = (f32[384,768]{1,0:T(8,128)}, f32[384,768]{1,0:T(8,128)}, u32[]{:S(2)}, u32[]{:S(2)}) collective-permute-start(f32[384,768]{1,0:T(8,128)} %convert_add_fusion.1), channel_id=1, source_target_pairs={{0,4},{4,0},{8,12},{12,8},{16,20},{20,16},{24,28},{28,24},{1,5},{5... | collective-permute-start | bytes 3538952 | tf_op jit(solution)/shard_map/ppermute | solution.py:31
  (114 other events, 1678.9 us)
Sparse Core Ops, SparseCore 0:
  19.1 59.3 all-gather.10
  80.1 28.5 all-gather.6
  110.9 49.5 all-gather.8
  161.9 49.2 all-gather.12
  235.6 23.9 reduce-scatter.6
  262.3 48.6 reduce-scatter.8
  313.9 48.0 reduce-scatter.10
  399.3 34.0 reduce-scatter.4

commit v2 on v1

v2 whole, which is shorter than its diff:
```python
import functools

import jax
import jax.numpy as jnp
from jax import lax
from jax.experimental import pallas as pl
from jax.experimental.pallas import tpu as pltpu
from jax.sharding import PartitionSpec as P

HEADS = 12
HEAD = 64
TILE = 512
EXP2_SCALE = 0.125 * 1.4426950408889634
f32 = jnp.float32
bf16 = jnp.bfloat16
VMEM_LIMIT = 56 * 1024 * 1024


def normalized(values):
    centered = values - jnp.mean(values, axis=-1, keepdims=True)
    variance = jnp.mean(centered * centered, axis=-1, keepdims=True)
    return centered * lax.rsqrt(variance + 1e-05)


def layer_norm(values, gain, shift):
    return normalized(values) * gain + shift


def gelu_tanh(values):
    return jax.nn.gelu(values, approximate=True)


def swapped(block, bit):
    n = lax.axis_size("ctx")
    return lax.ppermute(block, "ctx", [(i, i ^ (1 << bit)) for i in range(n)])


def sent_up(block, apart, up):
    n = lax.axis_size("ctx")
    pairs = [(i, i ^ apart) for i in range(n) if (i < i ^ apart) == up]
    return lax.ppermute(block, "ctx", pairs)


def mirrored(block):
    n = lax.axis_size("ctx")
    return lax.ppermute(block, "ctx", [(i, n - 1 - i) for i in range(n)])


def shifted(block, distance):
    n = lax.axis_size("shard")
    return lax.ppermute(block, "shard", [(i, (i + distance) % n) for i in range(n)])


def dot(a, b, contract):
    return lax.dot_general(a, b, ((contract[0], contract[1]), ((), ())), preferred_element_type=f32)


def rolled(block, start):
    return lax.dynamic_slice_in_dim(jnp.concatenate([block, block]), start, block.shape[0], 0)


def gather_small(block):
    n = lax.axis_size("shard")
    me = lax.axis_index("shard")
    held = jnp.stack([shifted(block, d) for d in range(n - 1, 0, -1)] + [block])
    return rolled(held, n - 1 - me)


def reduce_small(parts):
    n = lax.axis_size("shard")
    me = lax.axis_index("shard")
    total = lax.dynamic_index_in_dim(parts, me, 0, False)
    for d in range(1, n):
        total = total + shifted(lax.dynamic_index_in_dim(parts, (me + d) % n, 0, False), d)
    for bit in range(lax.axis_size("ctx").bit_length() - 1):
        total = total + swapped(total, bit)
    return total


def summed_over_chips(part, bits):
    for bit in bits:
        low = part.astype(bf16)
        part = low.astype(f32) + swapped(low, bit).astype(f32)
    return part


def pair_joined(half, odd):
    other = swapped(half, 0)
    return jnp.where(odd, other, half), jnp.where(odd, half, other)


def places(count, piece, shards, shard_at, axis):
    shape = (count, 1) if axis == 0 else (1, count)
    index = lax.broadcasted_iota(jnp.int32, shape, axis)
    owner = shard_at - index // piece
    owner = jnp.where(owner < 0, owner + shards, owner)
    return owner * piece + index % piece


def load_blocks(refs, held, sems):
    copies = [pltpu.make_async_copy(ref, held.at[i], sems.at[i]) for i, ref in enumerate(refs)]
    for copy in copies:
        copy.start()
    return copies


def forward_kernel(heads, shards, count, slots, info, q_ref, *refs):
    kv_refs = refs[:count]
    att_ref, out_ref, lse_ref, held, sems, m_ref, l_ref, acc_ref = refs[count:]
    rows, width = q_ref.shape
    piece = rows // shards
    tile = min(TILE, rows)
    per = rows // tile
    copies = load_blocks(kv_refs, held, sems)
    key_places = places(rows, piece, shards, info[1], 0)
    query_places = places(rows, piece, shards, info[1], 1)
    for copy in copies:
        copy.wait()
    for part in range(per):
        span = slice(part * tile, (part + 1) * tile)

        def step(slot, key_part, masked, start):
            keys_at = slice(key_part * tile, (key_part + 1) * tile)
            allowed = key_places[keys_at] <= query_places[:, span] if masked else None
            for h in range(heads):
                lanes = slice(h * HEAD, (h + 1) * HEAD)
                lanes_v = slice(width + h * HEAD, width + (h + 1) * HEAD)
                q = q_ref[span, lanes]
                k = held[slot, keys_at, lanes]
                v = held[slot, keys_at, lanes_v]
                s = dot(k, q, ((1,), (1,))) * EXP2_SCALE
                if masked:
                    s = jnp.where(allowed, s, -1e30)
                m = jnp.max(s, axis=0, keepdims=True)
                if start:
                    p = jnp.exp2(s - m)
                    l_ref[h] = jnp.sum(p, axis=0, keepdims=True)
                    acc_ref[h] = dot(v, p.astype(bf16), ((0,), (0,)))
                else:
                    old = m_ref[h]
                    m = jnp.maximum(old, m)
                    p = jnp.exp2(s - m)
                    factor = jnp.exp2(old - m)
                    l_ref[h] = l_ref[h] * factor + jnp.sum(p, axis=0, keepdims=True)
                    acc_ref[h] = acc_ref[h] * factor + dot(v, p.astype(bf16), ((0,), (0,)))
                m_ref[h] = m

        for key_part in range(per):
            step(slots[info[0]], key_part, True, key_part == 0)

        @pl.loop(0, info[0])
        def _(j):
            for key_part in range(per):
                step(slots[j], key_part, False, False)

        for h in range(heads):
            total = l_ref[h]
            done = acc_ref[h] / total
            out_ref[h * HEAD : (h + 1) * HEAD, span] = done
            lse_ref[h, :, span] = m_ref[h] + jnp.log2(total)
            low = done.astype(bf16)
            for z in range(tile // piece):
                att_ref[part * (tile // piece) + z, h * HEAD : (h + 1) * HEAD, :] = low[
                    :, z * piece : (z + 1) * piece
                ]


def backward_kernel(heads, shards, count, slots, info, q_ref, out_ref, lse_ref, *refs):
    go_refs = refs[:shards]
    kv_refs = refs[shards : shards + count]
    dq_ref, near_ref, far_ref, held, sums, sems, end_sems, acc_ref = refs[shards + count :]
    rows, width = q_ref.shape
    piece = rows // shards
    tile = min(TILE, rows)
    per = rows // tile
    copies = load_blocks(kv_refs, held, sems)
    key_places = places(rows, piece, shards, info[1], 0)
    query_places = places(rows, piece, shards, info[1], 1)

    @pl.loop(info[0] + 1, count)
    def _(j):
        sums[slots[j]] = jnp.zeros((rows, 2 * width), bf16)

    for copy in copies:
        copy.wait()
    for part in range(per):
        span = slice(part * tile, (part + 1) * tile)
        pieces = range(part * (tile // piece), (part + 1) * (tile // piece))
        go_all = jnp.concatenate([go_refs[z][...] for z in pieces], axis=1)
        deltas = []
        for h in range(heads):
            lanes = slice(h * HEAD, (h + 1) * HEAD)
            deltas.append(
                jnp.sum(go_all[lanes].astype(f32) * out_ref[lanes, span], axis=0, keepdims=True)
            )

        def step(slot, key_part, masked, start):
            keys_at = slice(key_part * tile, (key_part + 1) * tile)
            allowed = key_places[keys_at] <= query_places[:, span] if masked else None
            for h in range(heads):
                lanes = slice(h * HEAD, (h + 1) * HEAD)
                lanes_v = slice(width + h * HEAD, width + (h + 1) * HEAD)
                q = q_ref[span, lanes]
                go = go_all[lanes]
                k = held[slot, keys_at, lanes]
                v = held[slot, keys_at, lanes_v]
                p = jnp.exp2(dot(k, q, ((1,), (1,))) * EXP2_SCALE - lse_ref[h, :, span])
                if masked:
                    p = jnp.where(allowed, p, 0.0)
                pulled = dot(v, go, ((1,), (0,)))
                slopes = (p * (pulled - deltas[h])).astype(bf16)
                dv = dot(p.astype(bf16), go, ((1,), (1,)))
                dk = dot(slopes, q, ((1,), (0,))) * 0.125
                if part:
                    dk = dk + sums[slot, keys_at, lanes].astype(f32)
                    dv = dv + sums[slot, keys_at, lanes_v].astype(f32)
                sums[slot, keys_at, lanes] = dk.astype(bf16)
                sums[slot, keys_at, lanes_v] = dv.astype(bf16)
                dq = dot(k, slopes, ((0,), (0,)))
                if start:
                    acc_ref[h] = dq
                else:
                    acc_ref[h] += dq

        for key_part in range(per):
            step(slots[info[0]], key_part, True, key_part == 0)

        @pl.loop(0, info[0])
        def _(j):
            for key_part in range(per):
                step(slots[j], key_part, False, False)

        for h in range(heads):
            dq_ref[span, h * HEAD : (h + 1) * HEAD] = (acc_ref[h] * 0.125).T.astype(bf16)
    half = count // 2
    out_near = pltpu.make_async_copy(sums.at[pl.ds(0, half)], near_ref, end_sems.at[0])
    out_far = pltpu.make_async_copy(sums.at[pl.ds(half, half)], far_ref, end_sems.at[1])
    out_near.start()
    out_far.start()
    out_near.wait()
    out_far.wait()


SMEM = pl.BlockSpec(memory_space=pltpu.SMEM)
VMEM = pl.BlockSpec(memory_space=pltpu.VMEM)
ANY = pl.BlockSpec(memory_space=pl.ANY)


def attend(shards, slots, info, queries, blocks):
    rows, width = queries.shape
    heads = width // HEAD
    count = len(blocks)
    tile = min(TILE, rows)
    scores = heads * rows * rows * (count + 1) // 2
    return pl.pallas_call(
        functools.partial(forward_kernel, heads, shards, count),
        out_shape=(
            jax.ShapeDtypeStruct((shards, width, rows // shards), bf16),
            jax.ShapeDtypeStruct((width, rows), f32),
            jax.ShapeDtypeStruct((heads, 1, rows), f32),
        ),
        in_specs=[SMEM, SMEM, VMEM] + [ANY] * count,
        out_specs=(VMEM, VMEM, VMEM),
        scratch_shapes=[
            pltpu.VMEM((count, rows, 2 * width), bf16),
            pltpu.SemaphoreType.DMA((count,)),
            pltpu.VMEM((heads, 1, tile), f32),
            pltpu.VMEM((heads, 1, tile), f32),
            pltpu.VMEM((heads, HEAD, tile), f32),
        ],
        compiler_params=pltpu.CompilerParams(vmem_limit_bytes=VMEM_LIMIT),
        cost_estimate=pl.CostEstimate(
            flops=scores * 16 * HEAD,
            bytes_accessed=4 * rows * width * (count + 2),
            transcendentals=scores,
        ),
        name="attention_forward",
    )(slots, info, queries, *blocks)


def attend_back(shards, slots, info, queries, out, lse, grads, blocks):
    rows, width = queries.shape
    heads = width // HEAD
    count = len(blocks)
    tile = min(TILE, rows)
    scores = heads * rows * rows * (count + 1) // 2
    part = jax.ShapeDtypeStruct((count // 2, rows, 2 * width), bf16)
    return pl.pallas_call(
        functools.partial(backward_kernel, heads, shards, count),
        out_shape=(jax.ShapeDtypeStruct((rows, width), bf16), part, part),
        in_specs=[SMEM, SMEM, VMEM, VMEM, VMEM] + [VMEM] * shards + [ANY] * count,
        out_specs=(VMEM, ANY, ANY),
        scratch_shapes=[
            pltpu.VMEM((count, rows, 2 * width), bf16),
            pltpu.VMEM((count, rows, 2 * width), bf16),
            pltpu.SemaphoreType.DMA((count,)),
            pltpu.SemaphoreType.DMA((2,)),
            pltpu.VMEM((heads, HEAD, tile), f32),
        ],
        compiler_params=pltpu.CompilerParams(vmem_limit_bytes=VMEM_LIMIT),
        cost_estimate=pl.CostEstimate(
            flops=scores * 40 * HEAD,
            bytes_accessed=8 * rows * width * (count + 2),
            transcendentals=scores,
        ),
        name="attention_backward",
    )(slots, info, queries, out, lse, *grads, *blocks)


def body(
    layer_input,
    attn_gain,
    attn_shift,
    qkv_weight,
    query_bias,
    value_bias,
    proj_weight,
    proj_bias,
    mlp_gain,
    mlp_shift,
    fc_weight,
    fc_bias,
    out_weight,
    out_bias,
    grad_output,
):
    seqs, piece, width = layer_input.shape
    cycle = lax.axis_size("ctx")
    shards = lax.axis_size("shard")
    here = lax.axis_index("ctx")
    shard_at = lax.axis_index("shard")
    odd = here % 2
    chip_bits = list(range(1, cycle.bit_length() - 1))
    rows = shards * piece
    local_width = qkv_weight.shape[0]
    local_hidden = out_weight.shape[0]
    half_width = local_width // 2
    half_hidden = local_hidden // 2
    group = -(-HEADS // shards) * HEAD
    padded = group * shards
    late = [seq >= (seqs + 1) // 2 for seq in range(seqs)]
    tokens = seqs * piece

    def by_heads(weight):
        parts = []
        for third in range(3):
            part = weight[:, third * width : (third + 1) * width]
            parts.append(jnp.pad(part, ((0, 0), (0, padded - width))))
        return jnp.stack(
            [
                jnp.concatenate([part[:, z * group : (z + 1) * group] for part in parts], axis=1)
                for z in range(shards)
            ]
        )

    weight_half = lax.dynamic_slice_in_dim(qkv_weight, odd * half_width, half_width, 0)
    moved = lax.all_to_all(by_heads(weight_half), "shard", 0, 0, tiled=True)
    qkv_own = jnp.stack(pair_joined(moved, odd), axis=1).reshape(width, 3 * group)
    q_weight = qkv_own[:, :group]
    kv_weight = qkv_own[:, group:]

    packed = jnp.concatenate(
        [
            jnp.stack(
                [attn_gain, attn_shift, query_bias, value_bias, proj_bias, mlp_gain, mlp_shift, out_bias]
            ),
            fc_bias.reshape(-1, local_width),
        ]
    )
    small = gather_small(packed).astype(f32)
    vectors = [small[:, i].reshape(-1) for i in range(8)]
    gain_one, shift_one, query_add, value_add, proj_add, gain_two, shift_two, out_add = vectors
    fc_add = lax.dynamic_index_in_dim(
        small[:, 8:].reshape(shards, 2, half_hidden), odd, 1, False
    ).reshape(-1)

    def own_heads(vector):
        return lax.dynamic_slice_in_dim(
            jnp.pad(vector, (0, padded - width)), shard_at * group, group, 0
        )

    kv_add = jnp.concatenate([jnp.zeros((group,), f32), own_heads(value_add)])
    query_add = own_heads(query_add)

    proj_full = lax.all_gather(proj_weight, "shard", axis=0, tiled=True)
    fc_half = lax.all_gather(
        jnp.concatenate(
            [
                lax.dynamic_slice_in_dim(
                    fc_weight, z * local_hidden + odd * half_hidden, half_hidden, 1
                )
                for z in range(shards)
            ],
            axis=1,
        ),
        "shard",
        axis=0,
        tiled=True,
    )
    out_half = lax.all_gather(
        lax.dynamic_slice_in_dim(out_weight, odd * half_hidden, half_hidden, 0),
        "shard",
        axis=0,
        tiled=True,
    )
    proj_heads = rolled(
        jnp.pad(proj_full, ((0, padded - width), (0, 0))).reshape(shards, group, width), shard_at
    ).reshape(padded, width)

    inputs = [mirrored(layer_input[s]) if late[s] else layer_input[s] for s in range(seqs)]
    block_index = [cycle - 1 - here if late[s] else here for s in range(seqs)]
    group_norms, normed_one, queries, blocks, slots, infos = [], [], [], [], [], []
    for s in range(seqs):
        held = jnp.concatenate([inputs[s]] + [shifted(inputs[s], d) for d in range(1, shards)])
        norm = normalized(held.astype(f32))
        normed = (norm * gain_one + shift_one).astype(bf16)
        group_norms.append(norm)
        normed_one.append(normed)
        queries.append((dot(normed, q_weight, ((1,), (0,))) + query_add).astype(bf16))
        own = (dot(normed, kv_weight, ((1,), (0,))) + kv_add).astype(bf16)
        near = [own] + [sent_up(own, 2 * i, not late[s]) for i in range(1, cycle // 2)]
        blocks.append(near + [swapped(block, 0) for block in near])
        owners = jnp.arange(cycle)
        apart = (cycle - 1 - owners if late[s] else owners) ^ here
        slots.append(((apart >> 1) + (apart & 1) * (cycle // 2)).astype(jnp.int32))
        infos.append(jnp.stack([block_index[s], shard_at]).astype(jnp.int32))
    saved = []
    attended_parts = []
    for s in range(seqs):
        att, out, lse = attend(shards, slots[s], infos[s], queries[s], blocks[s])
        saved.append((out, lse))
        attended_parts.append(
            jnp.concatenate([att[0]] + [shifted(att[d], -d) for d in range(1, shards)])
        )
    attended = jnp.concatenate(attended_parts, axis=1)

    inputs32 = jnp.concatenate(inputs).astype(f32)
    grads_own = jnp.concatenate(
        [mirrored(grad_output[s]) if late[s] else grad_output[s] for s in range(seqs)]
    )
    grads32 = grads_own.astype(f32)
    middle = inputs32 + dot(attended, proj_heads, ((0,), (0,))) + proj_add
    normed_two = layer_norm(middle, gain_two, shift_two).astype(bf16)

    normed_pair = jnp.concatenate([normed_two, swapped(normed_two, 0)])
    grads_pair = jnp.concatenate([grads_own, swapped(grads_own, 0)])
    preactivation = dot(normed_pair, fc_half, ((1,), (0,))) + fc_add
    hidden = gelu_tanh(preactivation).astype(bf16)
    out_part = dot(hidden, out_half, ((1,), (0,)))
    layer_output = middle + (out_part[:tokens] + swapped(out_part[tokens:], 0)) + out_add
    layer_output = layer_output.astype(bf16)
    grad_hidden = dot(grads_pair, out_half, ((1,), (1,)))
    grad_pre = jax.vjp(gelu_tanh, preactivation)[1](grad_hidden)[0].astype(bf16)
    normed_part = dot(grad_pre, fc_half, ((1,), (1,)))
    grad_normed_two = normed_part[:tokens] + swapped(normed_part[tokens:], 0)
    grad_mid_part, gain_two_grad, shift_two_grad = jax.vjp(
        layer_norm, middle, gain_two, shift_two
    )[1](grad_normed_two)
    grad_middle = grads32 + grad_mid_part
    grad_branch = grad_middle.astype(bf16)

    grad_attended = dot(proj_heads, grad_branch, ((1,), (1,))).astype(bf16)
    query_low = [None] * seqs
    kv_parts = [None] * seqs
    for s in reversed(range(seqs)):
        go = grad_attended[:, s * piece : (s + 1) * piece]
        go = [go[e * group : (e + 1) * group] for e in range(shards)]
        go = [go[0]] + [shifted(go[e], e) for e in range(1, shards)]
        out, lse = saved[s]
        query_low[s], near, far = attend_back(
            shards, slots[s], infos[s], queries[s], out, lse, go, blocks[s]
        )
        kv_parts[s] = near.astype(f32) + swapped(far, 0).astype(f32)
    kv_low = [None] * seqs
    input_grads = [None] * seqs
    gain_one_grad = jnp.zeros((width,), f32)
    shift_one_grad = jnp.zeros((width,), f32)
    for s in reversed(range(seqs)):
        total = kv_parts[s][0]
        for i in range(1, cycle // 2):
            total = total + sent_up(kv_parts[s][i].astype(bf16), 2 * i, late[s]).astype(f32)
        kv_low[s] = total.astype(bf16)
        part = dot(query_low[s], q_weight, ((1,), (1,))) + dot(kv_low[s], kv_weight, ((1,), (1,)))
        gain_one_grad = gain_one_grad + jnp.sum(part * group_norms[s], axis=0)
        shift_one_grad = shift_one_grad + jnp.sum(part, axis=0)
        low = part.astype(bf16)
        grad_normed = part[:piece]
        for d in range(1, shards):
            grad_normed = grad_normed + shifted(low[d * piece : (d + 1) * piece], -d).astype(f32)
        own = slice(s * piece, (s + 1) * piece)
        pull = jax.vjp(lambda v: normalized(v) * gain_one, inputs32[own])[1]
        result = (grad_middle[own] + pull(grad_normed)[0]).astype(bf16)
        input_grads[s] = mirrored(result) if late[s] else result
    layer_output = [
        mirrored(layer_output[s * piece : (s + 1) * piece])
        if late[s]
        else layer_output[s * piece : (s + 1) * piece]
        for s in range(seqs)
    ]

    def pair_split(grad):
        parts = grad.astype(bf16).reshape(shards, 2, half_width, -1)
        mine = lax.dynamic_index_in_dim(parts, odd, 1, False)
        sent = lax.dynamic_index_in_dim(parts, 1 - odd, 1, False)
        return (mine.astype(f32) + swapped(sent, 0).astype(f32)).astype(bf16)

    flat = ((0,), (0,))
    out_grad = lax.psum_scatter(
        dot(hidden, grads_pair, flat).astype(bf16).reshape(shards, half_hidden, width),
        "shard",
        scatter_dimension=0,
        tiled=False,
    )
    out_grad = jnp.concatenate(pair_joined(summed_over_chips(out_grad, chip_bits[::-1]), odd))
    fc_grad = lax.psum_scatter(
        dot(normed_pair, grad_pre, flat).astype(bf16).reshape(shards, local_width, -1),
        "shard",
        scatter_dimension=0,
        tiled=False,
    )
    fc_halves = pair_joined(summed_over_chips(fc_grad, chip_bits), odd)
    fc_grad = jnp.concatenate(
        [
            fc_halves[h][:, z * half_hidden : (z + 1) * half_hidden]
            for z in range(shards)
            for h in range(2)
        ],
        axis=1,
    )
    in_order = rolled(attended.reshape(shards, group, tokens), (shards - shard_at) % shards)
    proj_grad = lax.psum_scatter(
        pair_split(dot(in_order.reshape(padded, tokens)[:width], grad_branch, ((1,), (0,)))),
        "shard",
        scatter_dimension=0,
        tiled=False,
    )
    proj_grad = jnp.concatenate(pair_joined(summed_over_chips(proj_grad, chip_bits), odd))

    def head_columns(low):
        grad = dot(normed_one[0], low[0], flat)
        for s in range(1, seqs):
            grad = grad + dot(normed_one[s], low[s], flat)
        grad = lax.all_to_all(pair_split(grad), "shard", 0, 0, tiled=True)
        halves = pair_joined(summed_over_chips(grad, chip_bits), odd)
        full = jnp.concatenate(halves, axis=1)
        return [
            jnp.concatenate(
                [full[z, :, at * group : (at + 1) * group] for z in range(shards)], axis=1
            )[:, :width]
            for at in range(full.shape[2] // group)
        ]

    qkv_grad = jnp.concatenate(head_columns(query_low) + head_columns(kv_low), axis=1)

    fc_add_part = jnp.sum(grad_pre.astype(f32), axis=0).reshape(shards, 1, half_hidden)
    fc_add_part = jnp.where(jnp.arange(2)[None, :, None] == odd, fc_add_part, 0.0)

    def all_heads(vector):
        return lax.dynamic_update_slice_in_dim(
            jnp.zeros((padded,), f32), vector, shard_at * group, 0
        )[:width]

    query_sum = sum(jnp.sum(low.astype(f32), axis=0) for low in query_low)
    value_sum = sum(jnp.sum(low[:, group:].astype(f32), axis=0) for low in kv_low)
    sums = reduce_small(
        jnp.concatenate(
            [
                v.reshape(shards, -1)
                for v in (
                    gain_one_grad,
                    shift_one_grad,
                    all_heads(query_sum),
                    all_heads(value_sum),
                    jnp.sum(grad_branch.astype(f32), axis=0),
                    gain_two_grad,
                    shift_two_grad,
                    jnp.sum(grads32, axis=0),
                    fc_add_part,
                )
            ],
            axis=1,
        )
    )
    parts = [sums[i * local_width : (i + 1) * local_width] for i in range(8)]
    return (
        jnp.stack(layer_output),
        jnp.stack(input_grads),
        parts[0],
        parts[1],
        qkv_grad,
        parts[2],
        parts[3],
        proj_grad,
        parts[4],
        parts[5],
        parts[6],
        fc_grad,
        sums[8 * local_width :],
        out_grad,
        parts[7],
    )


def solution(mesh):
    tokens = P(None, ("ctx", "shard"), None)
    vector = P("shard")
    matrix = P("shard", None)
    return jax.shard_map(
        body,
        mesh=mesh,
        in_specs=(
            tokens,
            vector,
            vector,
            matrix,
            vector,
            vector,
            matrix,
            vector,
            vector,
            vector,
            matrix,
            vector,
            matrix,
            vector,
            tokens,
        ),
        out_specs=(
            tokens,
            tokens,
            vector,
            vector,
            matrix,
            vector,
            vector,
            matrix,
            vector,
            vector,
            vector,
            matrix,
            vector,
            matrix,
            vector,
        ),
        check_vma=False,
    )
```

time: 486 us -> 546 us (1.12)
  the two profiles are of different devices: /device:TPU:0 before, /device:TPU:27 now
where the time goes in v2:
time: 546 us; the launch traced here: 536 us
  starting transfers between devices  173 us (32%)
  waiting for transfers between devices  138 us (25%)
  other arithmetic  63.6 us (12%)
  Pallas kernels  53.2 us (10%)
  local copies, waits for them, and re-layouts  51.3 us (9%)
  matrix products  40.7 us (7%)
  between operations  16.6 us (3%)
    ppermute x30, starting transfers between devices, shifted(): lax.ppermute(block, 'shard', [(i, (i + distance) % n) for i in range(n)])  62.4 us
    ppermute x36, waiting for transfers between devices, swapped(): return lax.ppermute(block, 'ctx', [(i, i ^ 1 << bit) for i in range(n)])  54.4 us
    ppermute x30, waiting for transfers between devices, shifted(): lax.ppermute(block, 'shard', [(i, (i + distance) % n) for i in range(n)])  49 us
    dot_general x21, matrix products, dot(): lax.dot_general(a, b, ((contract[0], contract[1]), ((), ())), preferred_e...  40.7 us
    ppermute x12, starting transfers between devices, sent_up(): return lax.ppermute(block, 'ctx', pairs)  35.9 us
    ppermute x36, starting transfers between devices, swapped(): return lax.ppermute(block, 'ctx', [(i, i ^ 1 << bit) for i in range(n)])  33.9 us
    pallas_call x2, Pallas kernels, attend_back(): pl.pallas_call(functools.partial(backward_kernel, heads, shards, count),...  30.7 us
    pallas_call x2, Pallas kernels, attend(): pl.pallas_call(functools.partial(forward_kernel, heads, shards, count), o...  22.5 us
  transfers between devices with their start and end apart: 91, of which 25 were waited for; matrix products, arithmetic and copies ran while one was open for 24% of the time, Pallas kernels for 10%

profile of v2, /device:TPU:27, one launch (start us, length us, event | category | flops | bytes accessed | tf_op | source)
XLA Modules:
  0.0 535.6 jit_solution(5319979689722579858)
XLA Ops:
  17.4 6.6 %all-to-all-start = ((bf16[4,96,576]{2,1,0:T(8,128)(2,1)}), bf16[4,96,576]{2,1,0:T(8,128)(2,1)}, u32[]{:S(2)}, u32[]{:S(2)}) async-start(bf16[4,96,576]{2,1,0:T(8,128)(2,1)} %pad_maximum_fusion.10), calls=%async_computation | async-start | bytes 983040 | tf_op jit(solution)/shard_map/all_to_all | solution.py:357
  29.8 8.1 %collective-permute-done.2 = bf16[128,768]{1,0:T(8,128)(2,1)S(1)} collective-permute-done((bf16[128,768]{1,0:T(8,128)(2,1)S(1)}, bf16[128,768]{1,0:T(8,128)(2,1)S(1)}, u32[]{:S(2)}, u32[]{:S(2)}) %collective-permute-start.2) | collective-permute-done | bytes 196640 | tf_op jit(solution)/shard_map/ppermute | solution.py:51
  37.9 11.7 %collective-permute-done.1 = bf16[128,768]{1,0:T(8,128)(2,1)S(1)} collective-permute-done((bf16[128,768]{1,0:T(8,128)(2,1)S(1)}, bf16[128,768]{1,0:T(8,128)(2,1)S(1)}, u32[]{:S(2)}, u32[]{:S(2)}) %collective-permute-start.1) | collective-permute-done | bytes 196640 | tf_op jit(solution)/shard_map/ppermute | solution.py:51
  49.8 19.0 %collective-permute-start.20 = (bf16[128,768]{1,0:T(8,128)(2,1)S(1)}, bf16[128,768]{1,0:T(8,128)(2,1)S(1)}, u32[]{:S(2)}, u32[]{:S(2)}) collective-permute-start(bf16[128,768]{1,0:T(8,128)(2,1)S(1)} %collective-permute-done), channel_id=1, source_target_pairs={{0,3},{1,0},{2,1},{3,2},{4,7},{5,4},{6,5},{7,6},{8,11},{9,8},{10,9... | collective-permute-start | bytes 589832 | tf_op jit(solution)/shard_map/ppermute | solution.py:51
  71.9 12.0 %collective-permute-done.19 = bf16[128,768]{1,0:T(8,128)(2,1)S(1)} collective-permute-done((bf16[128,768]{1,0:T(8,128)(2,1)S(1)}, bf16[128,768]{1,0:T(8,128)(2,1)S(1)}, u32[]{:S(2)}, u32[]{:S(2)}) %collective-permute-start.19) | collective-permute-done | bytes 196640 | tf_op jit(solution)/shard_map/ppermute | solution.py:51
  110.1 6.2 %collective-permute-done.22.refs_2_.refs_6_ = bf16[512,384]{1,0:T(8,128)(2,1)} collective-permute-done((bf16[512,384]{1,0:T(8,128)(2,1)S(1)}, bf16[512,384]{1,0:T(8,128)(2,1)}, u32[]{:S(2)}, u32[]{:S(2)}) %collective-permute-start.22) | collective-permute-done | bytes 393248 | tf_op jit(solution)/shard_map/ppermute | solution.py:41
  128.8 12.1 %attention_forward.3 = (bf16[4,192,128]{2,1,0:T(8,128)(2,1)}, f32[192,512]{1,0:T(8,128)}, f32[3,1,512]{2,1,0:T(1,128)}) custom-call(s32[8]{0:T(128)} %multiply_add_fusion.3.slots, s32[2]{0:T(128)} %pad_add_fusion.1.info, bf16[512,192]{1,0:T(8,128)(2,1)} %fusion.28.q_ref, bf16[512,384]{1,0:T(8,128)(2,1)} %copy-done.94, ...), custom_call_target="tpu_custom_call" | custom-call | flops 3623878656 | bytes 3932160 | tf_op jit(solution)/shard_map/attention_forward/pallas_call | solution.py:255
  141.9 13.5 %collective-permute-start.30 = (bf16[192,128]{1,0:T(8,128)(2,1)S(1)}, bf16[192,128]{1,0:T(8,128)(2,1)S(1)}, u32[]{:S(2)}, u32[]{:S(2)}) collective-permute-start(bf16[192,128]{1,0:T(8,128)(2,1)S(1)} %get-tuple-element.158), channel_id=1, source_target_pairs={{0,1},{1,2},{2,3},{3,0},{4,5},{5,6},{6,7},{7,4},{8,9},{9,10},{10,1... | collective-permute-start | bytes 147464 | tf_op jit(solution)/shard_map/ppermute | solution.py:51
  157.8 10.4 %attention_forward.2 = (bf16[4,192,128]{2,1,0:T(8,128)(2,1)}, f32[192,512]{1,0:T(8,128)}, f32[3,1,512]{2,1,0:T(1,128)}) custom-call(s32[8]{0:T(128)} %multiply_add_fusion.4.slots, s32[2]{0:T(128)} %pad_add_fusion.info, bf16[512,192]{1,0:T(8,128)(2,1)} %fusion.27.q_ref, bf16[512,384]{1,0:T(8,128)(2,1)} %fusion.24.refs_0_.refs_4_, ...), custom_call_target="tpu_custom_call" | custom-call | flops 3623878656 | bytes 3932160 | tf_op jit(solution)/shard_map/attention_forward/pallas_call | solution.py:255
  174.8 6.9 %collective-permute-done.16 = bf16[192,128]{1,0:T(8,128)(2,1)S(1)} collective-permute-done((bf16[192,128]{1,0:T(8,128)(2,1)S(1)}, bf16[192,128]{1,0:T(8,128)(2,1)S(1)}, u32[]{:S(2)}, u32[]{:S(2)}) %collective-permute-start.16) | collective-permute-done | bytes 49184 | tf_op jit(solution)/shard_map/ppermute | solution.py:51
  199.0 6.5 %convert_reduce_fusion = (f32[1536]{0:T(1024)}, bf16[512,1536]{1,0:T(8,128)(2,1)S(1)}) fusion(f32[512,1536]{1,0:T(8,128)} %convolution_add_fusion, bf16[1536,768]{1,0:T(8,128)(2,1)} %all-gather.8.cloned.1.call-done, bf16[256,768]{1,0:T(8,128)(2,1)} %collective-permute-done.35, bf16[128,768]{1,0:T(8,128)(2,1)S(1)} %collective-permute-done.34, ...), kind=kOutput, calls=%fused_computation.12 | convolution fusion | flops 1227618816 | bytes 7870464 | tf_op jit(solution)/shard_map/dot_general | solution.py:55
  229.4 8.7 %reduce-scatter.8.cloned.1.call-start = ((), (), s32[]{:S(2)}) async-start(), calls=%async_computation.11 | async-start | bytes 2949120 | tf_op jit(solution)/shard_map/reduce_scatter | solution.py:508
  251.2 16.3 %attention_backward.3 = (bf16[512,192]{1,0:T(8,128)(2,1)}, bf16[4,512,384]{2,1,0:T(8,128)(2,1)}, bf16[4,512,384]{2,1,0:T(8,128)(2,1)}) custom-call(s32[8]{0:T(128)} %multiply_add_fusion.3.slots, s32[2]{0:T(128)} %pad_add_fusion.1.info, bf16[512,192]{1,0:T(8,128)(2,1)} %fusion.28.q_ref, f32[192,512]{1,0:T(8,128)} %get-tuple-element.34.out_ref, ...), custom_call_target="tpu_custom_call" | custom-call | flops 9059696640 | bytes 7864320 | tf_op jit(solution)/shard_map/attention_backward/pallas_call | solution.py:288
  269.5 14.4 %attention_backward.2 = (bf16[512,192]{1,0:T(8,128)(2,1)}, bf16[4,512,384]{2,1,0:T(8,128)(2,1)}, bf16[4,512,384]{2,1,0:T(8,128)(2,1)}) custom-call(s32[8]{0:T(128)} %multiply_add_fusion.4.slots, s32[2]{0:T(128)} %pad_add_fusion.info, bf16[512,192]{1,0:T(8,128)(2,1)} %fusion.27.q_ref, f32[192,512]{1,0:T(8,128)} %get-tuple-element.29.out_ref, ...), custom_call_target="tpu_custom_call" | custom-call | flops 9059696640 | bytes 7864320 | tf_op jit(solution)/shard_map/attention_backward/pallas_call | solution.py:288
  296.9 7.7 %all-to-all-start.1 = ((bf16[4,96,192]{2,1,0:T(8,128)(2,1)}), bf16[4,96,192]{2,1,0:T(8,128)(2,1)}, u32[]{:S(2)}, u32[]{:S(2)}) async-start(bf16[4,96,192]{2,1,0:T(8,128)(2,1)} %fusion.52), calls=%async_computation.1 | async-start | bytes 393216 | tf_op jit(solution)/shard_map/all_to_all | solution.py:543
  305.5 7.1 %all-to-all-done.1 = bf16[4,96,192]{2,1,0:T(8,128)(2,1)} async-done(((bf16[4,96,192]{2,1,0:T(8,128)(2,1)}), bf16[4,96,192]{2,1,0:T(8,128)(2,1)}, u32[]{:S(2)}, u32[]{:S(2)}) %all-to-all-start.1) | async-done | bytes 147488 | tf_op jit(solution)/shard_map/all_to_all | solution.py:543
  361.1 8.2 %collective-permute-start.52 = (bf16[512,384]{1,0:T(8,128)(2,1)S(1)}, bf16[512,384]{1,0:T(8,128)(2,1)S(1)}, u32[]{:S(2)}, u32[]{:S(2)}) collective-permute-start(bf16[512,384]{1,0:T(8,128)(2,1)S(1)} %get-tuple-element.85), channel_id=1, source_target_pairs={{0,16},{4,20},{8,24},{12,28},{1,17},{5,21},{9,25},{13,29},{2,18},{... | collective-permute-start | bytes 1179656 | tf_op jit(solution)/shard_map/ppermute | solution.py:41
  429.5 9.5 %collective-permute-done.55 = bf16[128,768]{1,0:T(8,128)(2,1)S(1)} collective-permute-done((bf16[128,768]{1,0:T(8,128)(2,1)S(1)}, bf16[128,768]{1,0:T(8,128)(2,1)S(1)}, u32[]{:S(2)}, u32[]{:S(2)}) %collective-permute-start.55) | collective-permute-done | bytes 196640 | tf_op jit(solution)/shard_map/ppermute | solution.py:51
  448.7 6.5 %all-to-all-done.2 = bf16[4,96,384]{2,1,0:T(8,128)(2,1)S(1)} async-done(((bf16[4,96,384]{2,1,0:T(8,128)(2,1)}), bf16[4,96,384]{2,1,0:T(8,128)(2,1)S(1)}, u32[]{:S(2)}, u32[]{:S(2)}) %all-to-all-start.2) | async-done | bytes 294944 | tf_op jit(solution)/shard_map/all_to_all | solution.py:543
  456.7 6.4 %collective-permute-done.69 = bf16[4,96,384]{2,1,0:T(8,128)(2,1)S(1)} collective-permute-done((bf16[4,96,384]{2,1,0:T(8,128)(2,1)S(1)}, bf16[4,96,384]{2,1,0:T(8,128)(2,1)S(1)}, u32[]{:S(2)}, u32[]{:S(2)}) %collective-permute-start.69) | collective-permute-done | bytes 294944 | tf_op jit(solution)/shard_map/ppermute | solution.py:35
  463.3 12.5 %collective-permute-done.76 = bf16[192,1536]{1,0:T(8,128)(2,1)S(1)} collective-permute-done((bf16[192,1536]{1,0:T(8,128)(2,1)}, bf16[192,1536]{1,0:T(8,128)(2,1)S(1)}, u32[]{:S(2)}, u32[]{:S(2)}) %collective-permute-start.76) | collective-permute-done | bytes 589856 | tf_op jit(solution)/shard_map/ppermute | solution.py:35
  483.5 11.1 %collective-permute-done.77 = bf16[192,1536]{1,0:T(8,128)(2,1)S(1)} collective-permute-done((bf16[192,1536]{1,0:T(8,128)(2,1)S(1)}, bf16[192,1536]{1,0:T(8,128)(2,1)S(1)}, u32[]{:S(2)}, u32[]{:S(2)}) %collective-permute-start.77) | collective-permute-done | bytes 589856 | tf_op jit(solution)/shard_map/ppermute | solution.py:35
  500.2 7.0 %collective-permute-done.79 = bf16[384,768]{1,0:T(8,128)(2,1)S(1)} collective-permute-done((bf16[384,768]{1,0:T(8,128)(2,1)}, bf16[384,768]{1,0:T(8,128)(2,1)S(1)}, u32[]{:S(2)}, u32[]{:S(2)}) %collective-permute-start.79) | collective-permute-done | bytes 589856 | tf_op jit(solution)/shard_map/ppermute | solution.py:35
  513.2 6.6 %collective-permute-done.80 = bf16[384,768]{1,0:T(8,128)(2,1)S(1)} collective-permute-done((bf16[384,768]{1,0:T(8,128)(2,1)S(1)}, bf16[384,768]{1,0:T(8,128)(2,1)S(1)}, u32[]{:S(2)}, u32[]{:S(2)}) %collective-permute-start.80) | collective-permute-done | bytes 589856 | tf_op jit(solution)/shard_map/ppermute | solution.py:35
  (594 shorter events, 284.2 us)
Async XLA Ops:
  7.2 165.6 %all-gather.4.cloned.1.call-start = ((), (), s32[]{:S(2)}) async-start(), calls=%async_computation.6 | async-start | bytes 1474560 | tf_op jit(solution)/shard_map/all_gather | solution.py:385
  8.0 186.0 %all-gather.6.cloned.1.call-start = ((), (), s32[]{:S(2)}) async-start(), calls=%async_computation.7 | async-start | bytes 2949120 | tf_op jit(solution)/shard_map/all_gather | solution.py:386
  17.4 67.0 %all-to-all-start = ((bf16[4,96,576]{2,1,0:T(8,128)(2,1)}), bf16[4,96,576]{2,1,0:T(8,128)(2,1)}, u32[]{:S(2)}, u32[]{:S(2)}) async-start(bf16[4,96,576]{2,1,0:T(8,128)(2,1)} %pad_maximum_fusion.10), calls=%async_computation | async-start | bytes 983040 | tf_op jit(solution)/shard_map/all_to_all | solution.py:357
  24.0 175.0 %all-gather.8.cloned.1.call-start = ((), (), s32[]{:S(2)}) async-start(), calls=%async_computation.8 | async-start | bytes 2949120 | tf_op jit(solution)/shard_map/all_gather | solution.py:400
  24.9 328.7 %reduce-scatter.4.cloned.1.call-start = ((), (), s32[]{:S(2)}) async-start(), calls=%async_computation.9 | async-start | bytes 737280 | tf_op jit(solution)/shard_map/reduce_scatter | solution.py:531
  25.0 24.6 %collective-permute-start.1 = (bf16[128,768]{1,0:T(8,128)(2,1)S(1)}, bf16[128,768]{1,0:T(8,128)(2,1)S(1)}, u32[]{:S(2)}, u32[]{:S(2)}) collective-permute-start(bf16[128,768]{1,0:T(8,128)(2,1)S(1)} %get-tuple-element.151), channel_id=1, source_target_pairs={{0,1},{1,2},{2,3},{3,0},{4,5},{5,6},{6,7},{7,4},{8,9},{9,10},{10,1... | collective-permute-start | bytes 589832 | tf_op jit(solution)/shard_map/ppermute | solution.py:51
  25.1 24.7 %collective-permute-start = (bf16[128,768]{1,0:T(8,128)(2,1)S(1)}, bf16[128,768]{1,0:T(8,128)(2,1)S(1)}, u32[]{:S(2)}, u32[]{:S(2)}) collective-permute-start(bf16[128,768]{1,0:T(8,128)(2,1)S(1)} %copy-done.61), channel_id=1, source_target_pairs={{0,28},{4,24},{8,20},{12,16},{16,12},{20,8},{24,4},{28,0},{1,29},{... | collective-permute-start | bytes 589832 | tf_op jit(solution)/shard_map/ppermute | solution.py:46
  121.8 33.6 %collective-permute-start.11 = (bf16[512,384]{1,0:T(8,128)(2,1)}, bf16[512,384]{1,0:T(8,128)(2,1)S(1)}, u32[]{:S(2)}, u32[]{:S(2)}) collective-permute-start(bf16[512,384]{1,0:T(8,128)(2,1)} %fusion.24.refs_0_.refs_4_), channel_id=1, source_target_pairs={{0,4},{4,0},{8,12},{12,8},{16,20},{20,16},{24,28},{28,24},{1,5},{5... | collective-permute-start | bytes 1179656 | tf_op jit(solution)/shard_map/ppermute | solution.py:35
  125.2 30.8 %collective-permute-start.12 = (bf16[512,384]{1,0:T(8,128)(2,1)}, bf16[512,384]{1,0:T(8,128)(2,1)S(1)}, u32[]{:S(2)}, u32[]{:S(2)}) collective-permute-start(bf16[512,384]{1,0:T(8,128)(2,1)} %collective-permute-done.8.refs_1_.refs_5_), channel_id=1, source_target_pairs={{0,4},{4,0},{8,12},{12,8},{16,20},{20,16},{24,28},{28,24},{1,5},{5... | collective-permute-start | bytes 1179656 | tf_op jit(solution)/shard_map/ppermute | solution.py:35
  127.2 29.0 %collective-permute-start.13 = (bf16[512,384]{1,0:T(8,128)(2,1)S(1)}, bf16[512,384]{1,0:T(8,128)(2,1)S(1)}, u32[]{:S(2)}, u32[]{:S(2)}) collective-permute-start(bf16[512,384]{1,0:T(8,128)(2,1)S(1)} %collective-permute-done.9.refs_2_.refs_6_), channel_id=1, source_target_pairs={{0,4},{4,0},{8,12},{12,8},{16,20},{20,16},{24,28},{28,24},{1,5},{5... | collective-permute-start | bytes 1179656 | tf_op jit(solution)/shard_map/ppermute | solution.py:35
  127.3 28.9 %collective-permute-start.14 = (bf16[512,384]{1,0:T(8,128)(2,1)S(1)}, bf16[512,384]{1,0:T(8,128)(2,1)S(1)}, u32[]{:S(2)}, u32[]{:S(2)}) collective-permute-start(bf16[512,384]{1,0:T(8,128)(2,1)S(1)} %collective-permute-done.10.refs_3_.refs_7_), channel_id=1, source_target_pairs={{0,4},{4,0},{8,12},{12,8},{16,20},{20,16},{24,28},{28,24},{1,5},{5... | collective-permute-start | bytes 1179656 | tf_op jit(solution)/shard_map/ppermute | solution.py:35
  141.9 30.5 %collective-permute-start.30 = (bf16[192,128]{1,0:T(8,128)(2,1)S(1)}, bf16[192,128]{1,0:T(8,128)(2,1)S(1)}, u32[]{:S(2)}, u32[]{:S(2)}) collective-permute-start(bf16[192,128]{1,0:T(8,128)(2,1)S(1)} %get-tuple-element.158), channel_id=1, source_target_pairs={{0,1},{1,2},{2,3},{3,0},{4,5},{5,6},{6,7},{7,4},{8,9},{9,10},{10,1... | collective-permute-start | bytes 147464 | tf_op jit(solution)/shard_map/ppermute | solution.py:51
  224.9 230.3 %reduce-scatter.6.cloned.1.call-start = ((), (), s32[]{:S(2)}) async-start(), calls=%async_computation.10 | async-start | bytes 2949120 | tf_op jit(solution)/shard_map/reduce_scatter | solution.py:515
  229.4 253.2 %reduce-scatter.8.cloned.1.call-start = ((), (), s32[]{:S(2)}) async-start(), calls=%async_computation.11 | async-start | bytes 2949120 | tf_op jit(solution)/shard_map/reduce_scatter | solution.py:508
  305.2 33.1 %collective-permute-start.40 = (bf16[4,512,384]{2,1,0:T(8,128)(2,1)}, bf16[4,512,384]{2,1,0:T(8,128)(2,1)}, u32[]{:S(2)}, u32[]{:S(2)}) collective-permute-start(bf16[4,512,384]{2,1,0:T(8,128)(2,1)} %get-tuple-element.33), channel_id=1, source_target_pairs={{0,4},{4,0},{8,12},{12,8},{16,20},{20,16},{24,28},{28,24},{1,5},{5... | collective-permute-start | bytes 4718600 | tf_op jit(solution)/shard_map/ppermute | solution.py:35
  343.0 27.0 %collective-permute-start.43 = (bf16[512,384]{1,0:T(8,128)(2,1)}, bf16[512,384]{1,0:T(8,128)(2,1)S(1)}, u32[]{:S(2)}, u32[]{:S(2)}) collective-permute-start(bf16[512,384]{1,0:T(8,128)(2,1)} %get-tuple-element.87), channel_id=1, source_target_pairs={{16,8},{20,12},{24,0},{28,4},{17,9},{21,13},{25,1},{29,5},{18,10},... | collective-permute-start | bytes 1179656 | tf_op jit(solution)/shard_map/ppermute | solution.py:41
  344.2 27.0 %collective-permute-start.42 = (bf16[512,384]{1,0:T(8,128)(2,1)}, bf16[512,384]{1,0:T(8,128)(2,1)}, u32[]{:S(2)}, u32[]{:S(2)}) collective-permute-start(bf16[512,384]{1,0:T(8,128)(2,1)} %get-tuple-element.88), channel_id=1, source_target_pairs={{16,0},{20,4},{24,8},{28,12},{17,1},{21,5},{25,9},{29,13},{18,2},{... | collective-permute-start | bytes 1179656 | tf_op jit(solution)/shard_map/ppermute | solution.py:41
  345.6 25.8 %collective-permute-start.41 = (bf16[512,384]{1,0:T(8,128)(2,1)}, bf16[512,384]{1,0:T(8,128)(2,1)}, u32[]{:S(2)}, u32[]{:S(2)}) collective-permute-start(bf16[512,384]{1,0:T(8,128)(2,1)} %get-tuple-element.86), channel_id=1, source_target_pairs={{8,0},{12,4},{24,16},{28,20},{9,1},{13,5},{25,17},{29,21},{10,2},{... | collective-permute-start | bytes 1179656 | tf_op jit(solution)/shard_map/ppermute | solution.py:41
  371.3 51.4 %collective-permute-start.74 = (bf16[96,768]{1,0:T(8,128)(2,1)}, bf16[96,768]{1,0:T(8,128)(2,1)}, u32[]{:S(2)}, u32[]{:S(2)}) collective-permute-start(bf16[96,768]{1,0:T(8,128)(2,1)} %add_convert_fusion.6), channel_id=1, source_target_pairs={{0,16},{4,20},{8,24},{12,28},{16,0},{20,4},{24,8},{28,12},{1,17},{... | collective-permute-start | bytes 442376 | tf_op jit(solution)/shard_map/ppermute | solution.py:35
  429.4 51.3 %collective-permute-start.75 = (f32[96,768]{1,0:T(8,128)}, f32[96,768]{1,0:T(8,128)}, u32[]{:S(2)}, u32[]{:S(2)}) collective-permute-start(f32[96,768]{1,0:T(8,128)} %convert_add_fusion.10), channel_id=1, source_target_pairs={{0,4},{4,0},{8,12},{12,8},{16,20},{20,16},{24,28},{28,24},{1,5},{5... | collective-permute-start | bytes 884744 | tf_op jit(solution)/shard_map/ppermute | solution.py:35
  477.8 30.5 %collective-permute-start.57 = (bf16[128,768]{1,0:T(8,128)(2,1)}, bf16[128,768]{1,0:T(8,128)(2,1)S(1)}, u32[]{:S(2)}, u32[]{:S(2)}) collective-permute-start(bf16[128,768]{1,0:T(8,128)(2,1)} %get-tuple-element.126), channel_id=1, source_target_pairs={{0,28},{4,24},{8,20},{12,16},{16,12},{20,8},{24,4},{28,0},{1,29},{... | collective-permute-start | bytes 589832 | tf_op jit(solution)/shard_map/ppermute | solution.py:46
  482.6 24.6 %collective-permute-start.79 = (bf16[384,768]{1,0:T(8,128)(2,1)}, bf16[384,768]{1,0:T(8,128)(2,1)S(1)}, u32[]{:S(2)}, u32[]{:S(2)}) collective-permute-start(bf16[384,768]{1,0:T(8,128)(2,1)} %bitcast.196), channel_id=1, source_target_pairs={{0,16},{4,20},{8,24},{12,28},{16,0},{20,4},{24,8},{28,12},{1,17},{... | collective-permute-start | bytes 1769480 | tf_op jit(solution)/shard_map/ppermute | solution.py:35
  482.7 26.4 %collective-permute-start.71 = (f32[4,96,384]{2,1,0:T(8,128)S(1)}, f32[4,96,384]{2,1,0:T(8,128)S(1)}, u32[]{:S(2)}, u32[]{:S(2)}) collective-permute-start(f32[4,96,384]{2,1,0:T(8,128)S(1)} %convert_add_fusion.7), channel_id=1, source_target_pairs={{0,4},{4,0},{8,12},{12,8},{16,20},{20,16},{24,28},{28,24},{1,5},{5... | collective-permute-start | bytes 1769480 | tf_op jit(solution)/shard_map/ppermute | solution.py:35
  495.7 27.6 %collective-permute-start.78 = (f32[192,1536]{1,0:T(8,128)}, f32[192,1536]{1,0:T(8,128)}, u32[]{:S(2)}, u32[]{:S(2)}) collective-permute-start(f32[192,1536]{1,0:T(8,128)} %convert_add_fusion.4), channel_id=1, source_target_pairs={{0,4},{4,0},{8,12},{12,8},{16,20},{20,16},{24,28},{28,24},{1,5},{5... | collective-permute-start | bytes 3538952 | tf_op jit(solution)/shard_map/ppermute | solution.py:35
  (185 other events, 2188.9 us)
Sparse Core Ops, SparseCore 0:
  9.6 56.3 all-gather.3
  68.1 55.1 all-gather.5
  125.4 58.8 all-gather.7
  225.0 19.6 reduce-scatter.3
  247.4 49.3 reduce-scatter.5
  299.6 49.0 reduce-scatter.7
